TPU v7x, 32 devices: a whole 2x2x4 slice. The times are simulated.
32 devices in a mesh: member: 8 (over z, core), state: 4 (over y, x).
Axes of the slice: x: 2, y: 2, z: 4, core: 2. Of those that a mesh axis runs over, the one named last changes fastest.
Arguments:
- prior_analyses: float32 [64, 256, 1024], P('member', 'state'), may hold values from -6 to 6
- smoothing_number: float32 [256, 1024], P('state'), may hold values from 0.08 to 0.24
- observations: float32 [3072], replicated, may hold values from -6 to 6
- obs_variance: float32 [3072], replicated, may hold values from 0.25 to 2
- obs_row: int32 [3072], replicated, may hold values from 0 to 255
- obs_col: int32 [3072], replicated, may hold values from 0 to 1023
- obs_radius: int32 [3072], replicated, may hold values from 32 to 127
- block_order: int32 [3072], replicated, may hold values from 0 to 3071, each once
Outputs:
- analysis: float32 [64, 256, 1024], P('member', 'state')
Inputs may be any that keep to these rules, and one draw needn't show every extreme that they name: `block_order`: every observation index appears exactly once.
All inputs are finite; a program needn't handle non-finite values.
Results may differ from a plain program's by a relative error of at most 0.0035.
Values sent between devices are 32-bit elements; how exact they have to be, the bound alone decides.
A program may use at most 64 MiB of HBM per device.

v0:
```python
import jax
import jax.numpy as jnp
from jax import lax
from jax.sharding import PartitionSpec as P

BLK = 512
NBLK = 6


spread_eps = 1e-06


def extended(shard, sides, width):
    for axis, dim in sides:
        peers, length = (lax.axis_size(axis), shard.shape[dim])
        up = [(i, (i + 1) % peers) for i in range(peers - 1)]
        down = [(j, i) for i, j in up]
        last = lax.slice_in_dim(shard, length - width, length, axis=dim)
        leading = lax.slice_in_dim(shard, 0, width, axis=dim)
        before = lax.ppermute(last, axis, up)
        after = lax.ppermute(leading, axis, down)
        shard = jnp.concatenate([before, shard, after], axis=dim)
    return shard


def advance(padded, spreading_coefficients):
    center = padded[:, 1:-1, :]
    vertical = padded[:, 2:, :] + padded[:, :-2, :]
    sideways = jnp.pad(center[:, :, 1:], ((0, 0), (0, 0), (0, 1))) + jnp.pad(
        center[:, :, :-1], ((0, 0), (0, 0), (1, 0))
    )
    return center + spreading_coefficients * (vertical + sideways - 4.0 * center)


def predicted_level(realization_vectors, spreading_coefficients):
    current = realization_vectors
    for step_index in range(2):
        padded = extended(current, (("state", 1),), 1)
        current = advance(padded, spreading_coefficients)
    return current


def increments(prior_values, value_array, variances):
    realization_vectors = prior_values.shape[0]
    prior_mean = jnp.mean(prior_values, axis=0)
    anomaly = prior_values - prior_mean
    spread = jnp.sum(anomaly * anomaly, axis=0) / (realization_vectors - 1) + spread_eps
    post_var = spread * variances / (spread + variances)
    posterior_average = post_var * (prior_mean / spread + value_array / variances)
    shrink = jnp.sqrt(variances / (variances + spread)) - 1.0
    increment = (posterior_average - prior_mean + shrink * anomaly).astype(jnp.bfloat16)
    return (anomaly.astype(jnp.bfloat16), increment, 1.0 / spread)


def taper_weight(cell_row, cell_col, obs_rows, obs_cols, radius):
    row_gap = cell_row[None, :] - obs_rows[:, None]
    col_gap = cell_col[None, :] - obs_cols[:, None]
    distance = (row_gap * row_gap + col_gap * col_gap).astype(jnp.float32)
    reach = radius.astype(jnp.float32)
    closeness = jnp.maximum(1.0 - distance / (reach * reach)[:, None], 0.0)
    return closeness * closeness


def linear_gain_fit(
    target, target_rows, target_cols, anomaly, increment, inverse, obs_rows, obs_cols, radius
):
    realization_vectors = target.shape[0]
    cell_mean = jnp.mean(target, axis=0)
    cell_anomaly = (target - cell_mean).astype(jnp.bfloat16)
    sub_size = min(anomaly.shape[1], 128)
    accumulated = jnp.zeros(target.shape, jnp.float32)
    for part_index in range(anomaly.shape[1] // sub_size):
        lower_end = part_index * sub_size
        upper_end = lower_end + sub_size
        covariance = lax.dot_general(
            anomaly[:, lower_end:upper_end],
            cell_anomaly,
            (((0,), (0,)), ((), ())),
            preferred_element_type=jnp.float32,
        ) / (realization_vectors - 1)
        weight = taper_weight(
            target_rows,
            target_cols,
            obs_rows[lower_end:upper_end],
            obs_cols[lower_end:upper_end],
            radius[lower_end:upper_end],
        )
        gain_tile = (weight * covariance * inverse[lower_end:upper_end, None]).astype(jnp.bfloat16)
        accumulated = accumulated + jnp.dot(
            increment[:, lower_end:upper_end], gain_tile, preferred_element_type=jnp.float32
        )
    return accumulated


def pick_values(cell_values, rows_wanted, cols_wanted, first_row, tile_rows, tile_cols):
    local_row = rows_wanted - first_row
    inside = (
        (local_row >= 0) & (local_row < tile_rows) & (cols_wanted >= 0) & (cols_wanted < tile_cols)
    )
    local_index = jnp.where(inside, local_row * tile_cols + cols_wanted, 0)
    return jnp.where(inside[None, :], jnp.take(cell_values, local_index, axis=1), 0.0)


def on_device(
    prior_analyses,
    smoothing_number,
    observations,
    obs_variance,
    obs_row,
    obs_col,
    obs_radius,
    block_order,
):
    realization_vectors = predicted_level(prior_analyses, smoothing_number)
    row_count = realization_vectors.shape[1]
    col_count = realization_vectors.shape[2]
    member_count = lax.axis_size("member")
    base_row = lax.axis_index("state") * row_count
    tile_data = lax.all_to_all(
        realization_vectors, "member", split_axis=1, concat_axis=0, tiled=True
    )
    tile_rows = row_count // member_count
    first_row = base_row + lax.axis_index("member") * tile_rows
    grid_point_total = tile_rows * col_count
    cell_values = tile_data.reshape(tile_data.shape[0], grid_point_total)
    position = jnp.arange(grid_point_total, dtype=jnp.int32)
    cell_row = first_row + position // col_count
    cell_col = position % col_count
    for block_index in range(NBLK):
        chosen = block_order[block_index * BLK : (block_index + 1) * BLK]
        block_rows = jnp.take(obs_row, chosen)
        block_cols = jnp.take(obs_col, chosen)
        block_radius = jnp.take(obs_radius, chosen)
        local_values = pick_values(
            cell_values, block_rows, block_cols, first_row, tile_rows, col_count
        )
        prior_values = lax.psum(local_values, ("member", "state"))
        anomaly, increment, inverse = increments(
            prior_values, jnp.take(observations, chosen), jnp.take(obs_variance, chosen)
        )
        cell_values = cell_values + linear_gain_fit(
            cell_values,
            cell_row,
            cell_col,
            anomaly,
            increment,
            inverse,
            block_rows,
            block_cols,
            block_radius,
        )
    result = cell_values.reshape(tile_data.shape)
    return lax.all_to_all(result, "member", split_axis=0, concat_axis=1, tiled=True)


def solution(mesh):
    in_specs = (P("member", "state", None), P("state", None), P(), P(), P(), P(), P(), P())
    out_specs = P("member", "state", None)
    return jax.shard_map(
        on_device, mesh=mesh, in_specs=in_specs, out_specs=out_specs, check_vma=False
    )
```

profile of v0, /device:TPU:0, one launch (start us, length us, event | category | flops | bytes accessed | tf_op | source)
XLA Modules:
  0.0 1187.6 jit_solution(11396176168441743626)
XLA Ops:
  140.1 45.9 %all-to-all-done = f32[8,64,1024]{2,0,1:T(8,128)S(1)} async-done(((f32[8,64,1024]{2,0,1:T(8,128)}), f32[8,64,1024]{2,0,1:T(8,128)S(1)}, u32[]{:S(2)}, u32[]{:S(2)}) %all-to-all-start) | async-done | bytes 2097184 | tf_op jit(solution)/shard_map/all_to_all | solution.py:119
  193.2 124.2 %all-reduce.11.cloned.1.call-done = f32[64,512]{0,1:T(8,128)} async-done(((f32[64,512]{0,1:T(8,128)}), f32[64,512]{0,1:T(8,128)}) %all-reduce.11.cloned.1.call-update) | async-done | bytes 131088 | tf_op jit(solution)/shard_map/psum | solution.py:137
  330.4 5.6 convolution_add_fusion.16
  336.0 5.7 fusion.292
  350.1 123.9 %all-reduce.13.cloned.1.call-done = f32[64,512]{0,1:T(8,128)} async-done(((f32[64,512]{0,1:T(8,128)}), f32[64,512]{0,1:T(8,128)}) %all-reduce.13.cloned.1.call-update) | async-done | bytes 131088 | tf_op jit(solution)/shard_map/psum | solution.py:137
  481.4 5.6 convolution_add_fusion.14
  487.0 5.6 convolution_add_fusion.13
  492.6 5.7 fusion.295
  506.7 123.9 %all-reduce.15.cloned.1.call-done = f32[64,512]{0,1:T(8,128)} async-done(((f32[64,512]{0,1:T(8,128)}), f32[64,512]{0,1:T(8,128)}) %all-reduce.15.cloned.1.call-update) | async-done | bytes 131088 | tf_op jit(solution)/shard_map/psum | solution.py:137
  638.1 5.6 convolution_add_fusion.11
  643.6 5.6 convolution_add_fusion.10
  649.2 5.6 fusion.298
  662.2 123.7 %all-reduce.17.cloned.1.call-done = f32[64,512]{0,1:T(8,128)} async-done(((f32[64,512]{0,1:T(8,128)}), f32[64,512]{0,1:T(8,128)}) %all-reduce.17.cloned.1.call-update) | async-done | bytes 131088 | tf_op jit(solution)/shard_map/psum | solution.py:137
  799.0 5.6 convolution_add_fusion.7
  804.5 5.7 fusion.301
  818.6 123.9 %all-reduce.19.cloned.1.call-done = f32[64,512]{0,1:T(8,128)} async-done(((f32[64,512]{0,1:T(8,128)}), f32[64,512]{0,1:T(8,128)}) %all-reduce.19.cloned.1.call-update) | async-done | bytes 131088 | tf_op jit(solution)/shard_map/psum | solution.py:137
  950.0 5.6 convolution_add_fusion.5
  955.5 5.6 convolution_add_fusion.4
  961.1 5.7 fusion.304
  975.2 124.1 %all-reduce.21.cloned.1.call-done = f32[64,512]{0,1:T(8,128)} async-done(((f32[64,512]{0,1:T(8,128)}), f32[64,512]{0,1:T(8,128)}) %all-reduce.21.cloned.1.call-update) | async-done | bytes 131088 | tf_op jit(solution)/shard_map/psum | solution.py:137
  1107.0 5.6 convolution_add_fusion.2
  1112.6 5.6 convolution_add_fusion.1
  1118.2 5.7 fusion.72
  1126.7 52.4 %all_to_all.33 = f32[64,8,1024]{2,1,0:T(8,128)S(1)} all-to-all(f32[64,8,1024]{2,1,0:T(8,128)S(1)} %bitcast.36), channel_id=1, replica_groups=mesh['member'=8,'state'=4] {'member'}, dimensions={0} | all-to-all | bytes 4194304 | tf_op jit(solution)/shard_map/all_to_all | solution.py:153
  (229 shorter events, 240.7 us)
Async XLA Ops:
  9.4 106.3 %collective-permute-start.1 = (f32[8,1,1024]{2,0,1:T(8,128)S(1)}, f32[8,1,1024]{2,0,1:T(8,128)S(1)}, u32[]{:S(2)}, u32[]{:S(2)}) collective-permute-start(f32[8,1,1024]{2,0,1:T(8,128)S(1)} %get-tuple-element.57), channel_id=1, source_target_pairs={{0,1},{1,2},{2,3},{4,5},{5,6},{6,7},{8,9},{9,10},{10,11},{12,13},{... | collective-permute-start | bytes 98312 | tf_op jit(solution)/shard_map/ppermute | solution.py:20
  14.2 101.4 %collective-permute-start = (f32[8,1,1024]{2,0,1:T(8,128)S(1)}, f32[8,1,1024]{2,0,1:T(8,128)S(1)}, u32[]{:S(2)}, u32[]{:S(2)}) collective-permute-start(f32[8,1,1024]{2,0,1:T(8,128)S(1)} %get-tuple-element.56), channel_id=1, source_target_pairs={{1,0},{2,1},{3,2},{5,4},{6,5},{7,6},{9,8},{10,9},{11,10},{13,12},{... | collective-permute-start | bytes 98312 | tf_op jit(solution)/shard_map/ppermute | solution.py:21
  62.8 74.2 %copy-start.15 = (pred[512]{0:T(512)(128)(4,1)}, pred[512]{0:T(512)(128)(4,1)S(1)}, u32[]{:S(2)}) copy-start(pred[512]{0:T(512)(128)(4,1)S(1)} %get-tuple-element.8) | copy-start | bytes 1540
  100.8 14.8 %copy-start.10 = (f32[64,1024]{1,0:T(8,128)S(1)}, f32[64,1024]{1,0:T(8,128)}, u32[]{:S(2)}) copy-start(f32[64,1024]{1,0:T(8,128)} %param.15) | copy-start | bytes 786436
  119.0 7.1 collective-permute-start.3
  123.6 6.2 collective-permute-start.2
  132.1 53.9 %all-to-all-start = ((f32[8,64,1024]{2,0,1:T(8,128)}), f32[8,64,1024]{2,0,1:T(8,128)S(1)}, u32[]{:S(2)}, u32[]{:S(2)}) async-start(f32[8,64,1024]{2,0,1:T(8,128)} %fusion.82), calls=%async_computation | async-start | bytes 4194304 | tf_op jit(solution)/shard_map/all_to_all | solution.py:119
  137.0 180.5 %all-reduce.11.cloned.1.call-start = ((), (), s32[]{:S(2)}) async-start(), calls=%async_computation.2 | async-start | bytes 524288 | tf_op jit(solution)/shard_map/psum | solution.py:137
  192.9 281.1 %all-reduce.13.cloned.1.call-start = ((), (), s32[]{:S(2)}) async-start(), calls=%async_computation.3 | async-start | bytes 524288 | tf_op jit(solution)/shard_map/psum | solution.py:137
  341.7 135.8 %copy-start.6 = (f32[64,8192]{1,0:T(8,128)S(1)}, f32[64,8192]{1,0:T(8,128)}, u32[]{:S(2)}) copy-start(f32[64,8192]{1,0:T(8,128)} %get-tuple-element.201) | copy-start | bytes 6291460
  349.8 280.7 %all-reduce.15.cloned.1.call-start = ((), (), s32[]{:S(2)}) async-start(), calls=%async_computation.4 | async-start | bytes 524288 | tf_op jit(solution)/shard_map/psum | solution.py:137
  498.3 135.8 %copy-start.7 = (f32[64,8192]{1,0:T(8,128)S(1)}, f32[64,8192]{1,0:T(8,128)}, u32[]{:S(2)}) copy-start(f32[64,8192]{1,0:T(8,128)} %get-tuple-element.203) | copy-start | bytes 6291460
  506.4 279.5 %all-reduce.17.cloned.1.call-start = ((), (), s32[]{:S(2)}) async-start(), calls=%async_computation.5 | async-start | bytes 524288 | tf_op jit(solution)/shard_map/psum | solution.py:137
  661.8 280.8 %all-reduce.19.cloned.1.call-start = ((), (), s32[]{:S(2)}) async-start(), calls=%async_computation.6 | async-start | bytes 524288 | tf_op jit(solution)/shard_map/psum | solution.py:137
  810.3 135.8 %copy-start.8 = (f32[64,8192]{1,0:T(8,128)S(1)}, f32[64,8192]{1,0:T(8,128)}, u32[]{:S(2)}) copy-start(f32[64,8192]{1,0:T(8,128)} %get-tuple-element.207) | copy-start | bytes 6291460
  818.4 281.0 %all-reduce.21.cloned.1.call-start = ((), (), s32[]{:S(2)}) async-start(), calls=%async_computation.7 | async-start | bytes 524288 | tf_op jit(solution)/shard_map/psum | solution.py:137
  966.8 134.8 %copy-start.13 = (f32[512]{0:T(512)S(1)}, f32[512]{0:T(512)}, u32[]{:S(2)}) copy-start(f32[512]{0:T(512)} %gather_fusion.34) | copy-start | bytes 6148
  966.8 134.8 %copy-start.14 = (f32[512]{0:T(512)S(1)}, f32[512]{0:T(512)}, u32[]{:S(2)}) copy-start(f32[512]{0:T(512)} %gather_fusion.33) | copy-start | bytes 6148
  966.9 134.8 %copy-start.16 = (pred[512]{0:T(512)(128)(4,1)S(1)}, pred[512]{0:T(512)(128)(4,1)}, u32[]{:S(2)}) copy-start(pred[512]{0:T(512)(128)(4,1)} %copy-done.15) | copy-start | bytes 1540
  966.9 136.1 %copy-start.9 = (f32[64,8192]{1,0:T(8,128)S(1)}, f32[64,8192]{1,0:T(8,128)}, u32[]{:S(2)}) copy-start(f32[64,8192]{1,0:T(8,128)} %get-tuple-element.209) | copy-start | bytes 6291460
  966.9 136.1 %copy-start.25 = (s32[128]{0:T(128)S(1)}, s32[128]{0:T(128)}, u32[]{:S(2)}) copy-start(s32[128]{0:T(128)} %get-tuple-element.101) | copy-start | bytes 1540
  966.9 136.1 %copy-start.26 = (s32[128]{0:T(128)S(1)}, s32[128]{0:T(128)}, u32[]{:S(2)}) copy-start(s32[128]{0:T(128)} %get-tuple-element.237) | copy-start | bytes 1540
  966.9 136.1 %copy-start.30 = (f32[128]{0:T(128)S(1)}, f32[128]{0:T(128)}, u32[]{:S(2)}) copy-start(f32[128]{0:T(128)} %get-tuple-element.109) | copy-start | bytes 1540
  1126.7 53.9 %copy-start.1 = (s32[3072]{0:T(1024)S(1)}, s32[3072]{0:T(1024)}, u32[]{:S(2)}) copy-start(s32[3072]{0:T(1024)} %param.20) | copy-start | bytes 36868
  (18 other events, 125.4 us)
Sparse Core Ops, SparseCore 0:
  193.0 124.3 all-reduce.10
  350.0 123.9 all-reduce.12
  506.5 123.9 all-reduce.14
  661.9 124.0 all-reduce.16
  818.5 123.9 all-reduce.18
  975.4 123.9 all-reduce.20
where the time goes:
time: 1190 us
  waiting for transfers between devices  793 us (67%)
  local copies, waits for them, and re-layouts  149 us (13%)
  matrix products  125 us (11%)
  blocking collectives  52.4 us (4%)
  other arithmetic  34.9 us (3%)
  starting transfers between devices  18.5 us (2%)
  between operations  14.9 us (1%)
    psum x6, waiting for transfers between devices, on_device(): prior_values = lax.psum(local_values, ('member', 'state'))  744 us
    dot_general x24, matrix products, linear_gain_fit(): jnp.dot(increment[:, lower_end:upper_end], gain_tile, preferred_element_t...  125 us
    all_to_all x1, blocking collectives, on_device(): lax.all_to_all(result, 'member', split_axis=0, concat_axis=1, tiled=True)  52.4 us
    all_to_all x1, waiting for transfers between devices, on_device(): lax.all_to_all(realization_vectors, 'member', split_axis=1, concat_axis=0...  45.9 us
  transfers between devices with their start and end apart: 11, of which 8 were waited for; matrix products, arithmetic and copies ran while one was open for 9% of the time, Pallas kernels for 0%

commit v1 on v0

v1 whole, which is shorter than its diff:
```python
import functools

import jax
import jax.numpy as jnp
from jax import lax
from jax.experimental import pallas as pl
from jax.experimental.pallas import tpu as pltpu
from jax.sharding import PartitionSpec as P

BLK = 512
NBLK = 6
LANES = 128
TILE = 256
EPS = 1e-06
MESH = pl.DeviceIdType.MESH
VMEM = pl.BlockSpec(memory_space=pltpu.VMEM)
SMEM = pl.BlockSpec(memory_space=pltpu.SMEM)


def forecast(u, coef):
    peers = lax.axis_size("state")
    up = [(i, i + 1) for i in range(peers - 1)]
    down = [(j, i) for i, j in up]
    rows = u.shape[1]
    both = jnp.concatenate([u, coef[None]], axis=0)
    before = lax.ppermute(both[:, rows - 2 :], "state", up)
    after = lax.ppermute(both[:, :2], "state", down)
    full = jnp.concatenate([before, both, after], axis=1)
    current, field = full[:-1], full[-1]
    for _ in range(2):
        center = current[:, 1:-1]
        field = field[1:-1]
        vertical = current[:, 2:] + current[:, :-2]
        sideways = jnp.pad(center[:, :, 1:], ((0, 0), (0, 0), (0, 1))) + jnp.pad(
            center[:, :, :-1], ((0, 0), (0, 0), (1, 0))
        )
        current = center + field * (vertical + sideways - 4.0 * center)
    return current


def pick_kernel(base_ref, row_ref, col_ref, field_ref, out_ref):
    rows, members, _ = field_ref.shape
    base = base_ref[0]
    lane = lax.broadcasted_iota(jnp.int32, (members, LANES), 1)

    def chunk(j, _):
        def step(t, acc):
            for i in range(8):
                at = t * 8 + i
                k = j * LANES + at
                local = row_ref[k] - base
                col = col_ref[k]
                inside = (local >= 0) & (local < rows)
                local = jnp.clip(local, 0, rows - 1)
                start = pl.multiple_of((col // LANES) * LANES, LANES)
                part = field_ref[local, :, pl.ds(start, LANES)]
                turned = pltpu.roll(part, (at - col + 8 * LANES * 64) % LANES, 1)
                target = jnp.where(inside, at, -1)
                acc = jnp.where(lane == target, turned, acc)
            return acc

        acc = lax.fori_loop(0, LANES // 8, step, jnp.zeros((members, LANES), jnp.float32))
        out_ref[:, pl.ds(pl.multiple_of(j * LANES, LANES), LANES)] = acc
        return 0

    lax.fori_loop(0, out_ref.shape[1] // LANES, chunk, 0)


def share_kernel(n_member, n_state, part_ref, out_ref, slots, send_s, recv_s, send_m, recv_m):
    mi = lax.axis_index("member")
    si = lax.axis_index("state")
    barrier = pltpu.get_barrier_semaphore()
    for d in range(1, n_state):
        peer = lax.rem(si + d, n_state)
        pl.semaphore_signal(barrier, inc=1, device_id=(mi, peer), device_id_type=MESH)
    for d in range(1, n_member):
        peer = lax.rem(mi + d, n_member)
        pl.semaphore_signal(barrier, inc=1, device_id=(peer, si), device_id_type=MESH)
    pl.semaphore_wait(barrier, n_state + n_member - 2)
    first = []
    for d in range(1, n_state):
        peer = lax.rem(si + d, n_state)
        copy = pltpu.make_async_remote_copy(
            src_ref=part_ref,
            dst_ref=slots.at[d - 1],
            send_sem=send_s.at[d - 1],
            recv_sem=recv_s.at[d - 1],
            device_id=(mi, peer),
            device_id_type=MESH,
        )
        copy.start()
        first.append(copy)
    total = part_ref[...]
    for d in range(1, n_state):
        first[d - 1].wait()
        total = total + slots[d - 1]
    out_ref[mi] = total
    second = []
    for d in range(1, n_member):
        peer = lax.rem(mi + d, n_member)
        copy = pltpu.make_async_remote_copy(
            src_ref=out_ref.at[mi],
            dst_ref=out_ref.at[mi],
            send_sem=send_m.at[d - 1],
            recv_sem=recv_m.at[d - 1],
            device_id=(peer, si),
            device_id_type=MESH,
        )
        copy.start()
        second.append(copy)
    for copy in second:
        copy.wait()


def assimilate_kernel(
    base_ref, x_ref, y0_ref, pcol_ref, prow_ref, out_ref, y_ref, near_ref, across_ref, ybt_ref, dy_ref, q_ref
):
    rows, members, cols = x_ref.shape
    base = base_ref[0].astype(jnp.float32)
    out_ref[...] = x_ref[...]
    y_ref[...] = y0_ref[...]
    groups = TILE // LANES

    def anomalies(values):
        return (values - jnp.mean(values, axis=0, keepdims=True)).astype(jnp.bfloat16)

    def block(b, _):
        own = pl.ds(pl.multiple_of(b * BLK, BLK), BLK)
        values = y_ref[:, own]
        mean = jnp.mean(values, axis=0, keepdims=True)
        anomaly = values - mean
        spread = jnp.sum(anomaly * anomaly, axis=0, keepdims=True) / (members - 1) + EPS
        observed = prow_ref[3:4, own]
        variance = prow_ref[4:5, own]
        post = spread * variance / (spread + variance)
        center = post * (mean / spread + observed / variance)
        shrink = jnp.sqrt(variance / (variance + spread)) - 1.0
        dy_ref[...] = (center - mean + shrink * anomaly).astype(jnp.bfloat16)
        turned = anomaly.T
        ybt_ref[...] = turned.astype(jnp.bfloat16)
        spread_c = jnp.sum(turned * turned, axis=1, keepdims=True) / (members - 1) + EPS
        q = jnp.sqrt(1.0 / (spread_c * (members - 1)))
        obs_r = pcol_ref[own, 0:1]
        obs_c = pcol_ref[own, 1:2]
        reach = pcol_ref[own, 2:3]
        inv = q / (reach * reach)
        q_ref[:, 0:1] = q
        q_ref[:, 1:2] = inv
        for r in range(rows):
            gap = base + float(r) - obs_r
            near_ref[r] = jnp.broadcast_to(q - gap * gap * inv, (BLK, LANES))

        def column(t, _):
            at = pl.ds(pl.multiple_of(t * TILE, TILE), TILE)
            place = (lax.broadcasted_iota(jnp.int32, (1, TILE), 1) + t * TILE).astype(jnp.float32)
            gap = place - obs_c
            across_ref[...] = gap * gap * inv

            def row(r, _):
                x = out_ref[r, :, at]
                cov = jnp.dot(ybt_ref[...], anomalies(x), preferred_element_type=jnp.float32)
                near = near_ref[r]
                near = jnp.concatenate([near] * groups, axis=1)
                w = jnp.maximum(near - across_ref[...], 0.0)
                gain = (w * w * cov).astype(jnp.bfloat16)
                out_ref[r, :, at] = x + jnp.dot(dy_ref[...], gain, preferred_element_type=jnp.float32)
                return 0

            lax.fori_loop(0, rows, row, 0)
            return 0

        lax.fori_loop(0, cols // TILE, column, 0)

        def later(t, _):
            at = pl.ds(pl.multiple_of(t * TILE, TILE), TILE)
            y = y_ref[:, at]
            cov = jnp.dot(ybt_ref[...], anomalies(y), preferred_element_type=jnp.float32)
            gap_r = prow_ref[0:1, at] - pcol_ref[own, 0:1]
            gap_c = prow_ref[1:2, at] - pcol_ref[own, 1:2]
            w = jnp.maximum(q_ref[:, 0:1] - (gap_r * gap_r + gap_c * gap_c) * q_ref[:, 1:2], 0.0)
            gain = (w * w * cov).astype(jnp.bfloat16)
            y_ref[:, at] = y + jnp.dot(dy_ref[...], gain, preferred_element_type=jnp.float32)
            return 0

        per = BLK // TILE
        lax.fori_loop((b + 1) * per, NBLK * per, later, 0)
        return 0

    lax.fori_loop(0, NBLK, block, 0)


def on_device(prior, coef, observations, obs_variance, obs_row, obs_col, obs_radius, block_order):
    n_member = lax.axis_size("member")
    n_state = lax.axis_size("state")
    local_members, local_rows, cols = prior.shape
    members = local_members * n_member
    n_obs = block_order.shape[0]
    f32 = jnp.float32
    table = jnp.stack(
        [
            obs_row.astype(f32),
            obs_col.astype(f32),
            obs_radius.astype(f32),
            observations,
            obs_variance,
        ]
        + [jnp.zeros((n_obs,), f32)] * 3,
        axis=1,
    )
    by_obs = jnp.take(table, block_order, axis=0)
    by_field = by_obs.T
    row_i = by_field[0].astype(jnp.int32)
    col_i = by_field[1].astype(jnp.int32)

    now = forecast(prior, coef).transpose(1, 0, 2)
    base_row = lax.axis_index("state") * local_rows
    tile_rows = local_rows // n_member
    first_row = base_row + lax.axis_index("member") * tile_rows
    cells = lax.all_to_all(now, "member", split_axis=0, concat_axis=1, tiled=True)

    part = pl.pallas_call(
        pick_kernel,
        out_shape=jax.ShapeDtypeStruct((local_members, n_obs), f32),
        in_specs=[SMEM, SMEM, SMEM, VMEM],
        out_specs=VMEM,
        compiler_params=pltpu.CompilerParams(vmem_limit_bytes=32 * 1024 * 1024),
        cost_estimate=pl.CostEstimate(flops=10**7, bytes_accessed=10**7, transcendentals=0),
    )(jnp.reshape(base_row, (1,)).astype(jnp.int32), row_i, col_i, now)
    shared = pl.pallas_call(
        functools.partial(share_kernel, n_member, n_state),
        out_shape=jax.ShapeDtypeStruct((n_member, local_members, n_obs), f32),
        in_specs=[VMEM],
        out_specs=VMEM,
        scratch_shapes=[
            pltpu.VMEM((n_state - 1, local_members, n_obs), f32),
            pltpu.SemaphoreType.DMA((n_state - 1,)),
            pltpu.SemaphoreType.DMA((n_state - 1,)),
            pltpu.SemaphoreType.DMA((n_member - 1,)),
            pltpu.SemaphoreType.DMA((n_member - 1,)),
        ],
        compiler_params=pltpu.CompilerParams(
            collective_id=0, has_side_effects=True, vmem_limit_bytes=32 * 1024 * 1024
        ),
    )(part)
    y0 = shared.reshape(members, n_obs)
    result = pl.pallas_call(
        assimilate_kernel,
        out_shape=jax.ShapeDtypeStruct(cells.shape, f32),
        in_specs=[SMEM, VMEM, VMEM, VMEM, VMEM],
        out_specs=VMEM,
        scratch_shapes=[
            pltpu.VMEM((members, n_obs), f32),
            pltpu.VMEM((tile_rows, BLK, LANES), f32),
            pltpu.VMEM((BLK, TILE), f32),
            pltpu.VMEM((BLK, members), jnp.bfloat16),
            pltpu.VMEM((members, BLK), jnp.bfloat16),
            pltpu.VMEM((BLK, LANES), f32),
        ],
        compiler_params=pltpu.CompilerParams(vmem_limit_bytes=48 * 1024 * 1024),
    )(jnp.reshape(first_row, (1,)).astype(jnp.int32), cells, y0, by_obs, by_field)
    back = lax.all_to_all(result, "member", split_axis=1, concat_axis=0, tiled=True)
    return back.transpose(1, 0, 2)


def solution(mesh):
    in_specs = (P("member", "state", None), P("state", None), P(), P(), P(), P(), P(), P())
    out_specs = P("member", "state", None)
    return jax.shard_map(
        on_device, mesh=mesh, in_specs=in_specs, out_specs=out_specs, check_vma=False
    )
```

time: 1190 us -> 296 us (0.25)
  waiting for transfers between devices: 793 us -> 6.19 us
  Pallas kernels: 0 us -> 184 us
  matrix products: 125 us -> 0 us
  local copies, waits for them, and re-layouts: 149 us -> 29.9 us
  other arithmetic: 34.9 us -> 6.66 us
  between operations: 14.9 us -> 0.29 us
    psum x6 -> x0, waiting for transfers between devices: 744 us -> none  [on_device(): prior_values = lax.psum(local_values, ('member', 'state'))]
    pallas_call x0 -> x3, Pallas kernels: none -> 184 us  [the longest x1 106 us: on_device(): pl.pallas_call(assimilate_kernel, out_shape=jax.ShapeDtypeStruct(cells.sh...]
    dot_general x24 -> x0, matrix products: 125 us -> none  [linear_gain_fit(): jnp.dot(increment[:, lower_end:upper_end], gain_tile, preferred_element_t...]
    gather x36 -> x2, local copies, waits for them, and re-layouts: 116 us -> 8.55 us  [on_device(): by_obs = jnp.take(table, block_order, axis=0)]
    all_to_all x1, waiting for transfers between devices: 45.9 us -> 0.01 us  [on_device(): lax.all_to_all(now, 'member', split_axis=0, concat_axis=1, tiled=True)]
    add x5 -> x0, local copies, waits for them, and re-layouts: 18.5 us -> none  [on_device(): cell_values + linear_gain_fit(cell_values, cell_row, cell_col, anomaly, i...]
    reduce_sum x13 -> x0, other arithmetic: 13.9 us -> none  [the longest x6 7.11 us: increments(): jnp.sum(anomaly * anomaly, axis=0) / (realization_vectors - 1) + spread_eps]
  transfers between devices with their start and end apart: 11 -> 3, of which waited for: 8 -> 2; matrix products, arithmetic and copies ran while one was open for 9% -> 3% of each run, Pallas kernels for 0% -> 26%
where the time goes in v1:
time: 296 us; the launch traced here: 295 us
  Pallas kernels  184 us (62%)
  blocking collectives  57.1 us (19%)
  local copies, waits for them, and re-layouts  29.9 us (10%)
  starting transfers between devices  11.2 us (4%)
  other arithmetic  6.66 us (2%)
  waiting for transfers between devices  6.19 us (2%)
    pallas_call x1, Pallas kernels, on_device(): pl.pallas_call(assimilate_kernel, out_shape=jax.ShapeDtypeStruct(cells.sh...  106 us
    all_to_all x1, blocking collectives, on_device(): lax.all_to_all(result, 'member', split_axis=1, concat_axis=0, tiled=True)  57.1 us
    pallas_call x1, Pallas kernels, on_device(): pl.pallas_call(pick_kernel, out_shape=jax.ShapeDtypeStruct((local_members...  54.2 us
    pallas_call x1, Pallas kernels, on_device(): pl.pallas_call(functools.partial(share_kernel, n_member, n_state), out_sh...  23.8 us
    gather x2, local copies, waits for them, and re-layouts, on_device(): by_obs = jnp.take(table, block_order, axis=0)  8.55 us
    concatenate x1, local copies, waits for them, and re-layouts, forecast(): both = jnp.concatenate([u, coef[None]], axis=0)  6.06 us
  transfers between devices with their start and end apart: 3, of which 2 were waited for; matrix products, arithmetic and copies ran while one was open for 3% of the time, Pallas kernels for 26%

profile of v1, /device:TPU:0, one launch (start us, length us, event | category | flops | bytes accessed | tf_op | source)
XLA Modules:
  0.0 295.4 jit_solution(5674337328337964658)
XLA Ops:
  0.0 4.2 %copy_dynamic-update-slice_fusion = f32[9,64,1024]{2,0,1:T(8,128)} fusion(f32[8,64,1024]{2,1,0:T(8,128)} %param.8), kind=kLoop, calls=%fused_computation.17 | loop fusion | bytes 4194304
  4.4 6.1 %dynamic-update-slice.1 = f32[9,64,1024]{2,0,1:T(8,128)} dynamic-update-slice(f32[9,64,1024]{2,0,1:T(8,128)} %copy_dynamic-update-slice_fusion, f32[1,64,1024]{2,0,1:T(1,128)S(1)} %broadcast_in_dim.17, s32[]{} %constant.49, s32[]{} %constant.48, s32[]{} %constant.48) | dynamic-update-slice | bytes 524292 | tf_op jit(solution)/shard_map/concatenate | solution.py:25
  10.5 1.0 fusion.12
  11.5 4.8 %collective-permute-start = (f32[9,2,1024]{2,0,1:T(8,128)S(1)}, f32[9,2,1024]{2,0,1:T(8,128)S(1)}, u32[]{:S(2)}, u32[]{:S(2)}) collective-permute-start(f32[9,2,1024]{2,0,1:T(8,128)S(1)} %get-tuple-element.8), channel_id=1, source_target_pairs={{0,1},{1,2},{2,3},{4,5},{5,6},{6,7},{8,9},{9,10},{10,11},{12,13},{... | collective-permute-start | bytes 221192 | tf_op jit(solution)/shard_map/ppermute | solution.py:26
  16.3 1.3 collective-permute-start.1
  17.6 1.4 collective-permute-done
  19.0 4.8 %collective-permute-done.1 = f32[9,2,1024]{2,0,1:T(8,128)S(1)} collective-permute-done((f32[9,2,1024]{2,0,1:T(8,128)S(1)}, f32[9,2,1024]{2,0,1:T(8,128)S(1)}, u32[]{:S(2)}, u32[]{:S(2)}) %collective-permute-start.1) | collective-permute-done | bytes 73760 | tf_op jit(solution)/shard_map/ppermute | solution.py:27
  23.8 2.7 pad_maximum_fusion
  26.5 0.9 fusion.11
  27.3 1.3 copy-done
  28.9 1.3 fusion.4
  30.3 0.7 fusion.13
  31.0 2.4 fusion.9.field_ref
  33.4 5.0 %all-to-all-start = ((f32[64,8,1024]{2,1,0:T(8,128)}), f32[64,8,1024]{2,1,0:T(8,128)}, u32[]{:S(2)}, u32[]{:S(2)}) async-start(f32[64,8,1024]{2,1,0:T(8,128)} %fusion.9.field_ref), calls=%async_computation | async-start | bytes 4194304 | tf_op jit(solution)/shard_map/all_to_all | solution.py:219
  38.7 0.5 copy.26
  39.2 8.1 %gather_fusion = f32[3072,8]{1,0:T(8,128)S(1)} fusion(f32[3072,8]{1,0:T(8,128)S(1)} %copy.26, s32[3072]{0:T(1024)S(1)} %fusion.10), kind=kCustom, calls=%fused_computation | custom fusion | bytes 208896 | tf_op jit(solution)/shard_map/jit(_take)/gather | solution.py:210
  47.8 0.5 copy.28.pcol_ref
  48.3 54.2 %shard_map.82.part_ref = f32[8,3072]{1,0:T(8,128)S(1)} custom-call(s32[1]{0:T(128)} %bitcast.5.base_ref, s32[3072]{0:T(1024)S(1)} %bitcast.33, s32[3072]{0:T(1024)S(1)} %bitcast.32, f32[64,8,1024]{2,1,0:T(8,128)} %fusion.9.field_ref), custom_call_target="tpu_custom_call" | custom-call | flops 10000000 | bytes 10000000 | tf_op jit(solution)/shard_map/pallas_call | solution.py:221
  102.5 23.8 %shard_map.83 = f32[8,8,3072]{2,1,0:T(8,128)S(1)} custom-call(f32[8,3072]{1,0:T(8,128)S(1)} %shard_map.82.part_ref), custom_call_target="tpu_custom_call" | custom-call | tf_op jit(solution)/shard_map/pallas_call | solution.py:229
  126.3 3.2 %copy.37 = f32[8,8,8,1024]{3,2,0,1:T(8,128)} copy(f32[8,8,8,1024]{3,2,1,0:T(8,128)} %bitcast.2) | data formatting | bytes 4194304 | tf_op jit(solution)/shard_map/all_to_all | solution.py:219
  129.5 106.1 %shard_map.84 = f32[8,64,1024]{2,1,0:T(8,128)S(1)} custom-call(s32[1]{0:T(128)} %bitcast.base_ref, f32[8,64,1024]{2,1,0:T(8,128)} %bitcast.34, f32[64,3072]{1,0:T(8,128)S(1)} %bitcast.31, f32[3072,8]{1,0:T(8,128)S(1)} %copy.28.pcol_ref, f32[8,3072]{1,0:T(8,128)S(1)} %fusion.14.prow_ref), custom_call_target="tpu_custom_call" | custom-call | tf_op jit(solution)/shard_map/pallas_call | solution.py:246
  235.6 1.2 copy.29
  236.8 57.1 %all_to_all.36 = f32[8,64,1024]{2,0,1:T(8,128)S(1)} all-to-all(f32[8,64,1024]{2,0,1:T(8,128)S(1)} %copy.29), channel_id=1, replica_groups=mesh['member'=8,'state'=4] {'member'}, dimensions={1} | all-to-all | bytes 4194304 | tf_op jit(solution)/shard_map/all_to_all | solution.py:261
  294.0 1.5 copy.36
  (31 shorter events, 1.2 us)
Async XLA Ops:
  0.0 4.2 %copy-start.1 = (f32[64,1024]{1,0:T(8,128)S(1)}, f32[64,1024]{1,0:T(8,128)}, u32[]{:S(2)}) copy-start(f32[64,1024]{1,0:T(8,128)} %param.9) | copy-start | bytes 786436
  11.5 7.6 %collective-permute-start = (f32[9,2,1024]{2,0,1:T(8,128)S(1)}, f32[9,2,1024]{2,0,1:T(8,128)S(1)}, u32[]{:S(2)}, u32[]{:S(2)}) collective-permute-start(f32[9,2,1024]{2,0,1:T(8,128)S(1)} %get-tuple-element.8), channel_id=1, source_target_pairs={{0,1},{1,2},{2,3},{4,5},{5,6},{6,7},{8,9},{9,10},{10,11},{12,13},{... | collective-permute-start | bytes 221192 | tf_op jit(solution)/shard_map/ppermute | solution.py:26
  16.3 7.5 %collective-permute-start.1 = (f32[9,2,1024]{2,0,1:T(8,128)S(1)}, f32[9,2,1024]{2,0,1:T(8,128)S(1)}, u32[]{:S(2)}, u32[]{:S(2)}) collective-permute-start(f32[9,2,1024]{2,0,1:T(8,128)S(1)} %get-tuple-element.7), channel_id=1, source_target_pairs={{1,0},{2,1},{3,2},{5,4},{6,5},{7,6},{9,8},{10,9},{11,10},{13,12},{... | collective-permute-start | bytes 221192 | tf_op jit(solution)/shard_map/ppermute | solution.py:27
  26.5 2.2 copy-start
  33.4 5.1 %copy-start.5 = (s32[3072]{0:T(1024)S(1)}, s32[3072]{0:T(1024)}, u32[]{:S(2)}) copy-start(s32[3072]{0:T(1024)} %param.12) | copy-start | bytes 36868
  33.4 5.1 %copy-start.6 = (s32[3072]{0:T(1024)S(1)}, s32[3072]{0:T(1024)}, u32[]{:S(2)}) copy-start(s32[3072]{0:T(1024)} %param.13) | copy-start | bytes 36868
  33.4 5.1 %copy-start.7 = (s32[3072]{0:T(1024)S(1)}, s32[3072]{0:T(1024)}, u32[]{:S(2)}) copy-start(s32[3072]{0:T(1024)} %param.14) | copy-start | bytes 36868
  33.4 5.1 %copy-start.3 = (f32[3072]{0:T(1024)S(1)}, f32[3072]{0:T(1024)}, u32[]{:S(2)}) copy-start(f32[3072]{0:T(1024)} %param.10) | copy-start | bytes 36868
  33.4 5.2 %copy-start.4 = (f32[3072]{0:T(1024)S(1)}, f32[3072]{0:T(1024)}, u32[]{:S(2)}) copy-start(f32[3072]{0:T(1024)} %param.11) | copy-start | bytes 36868
  33.4 5.8 %copy-start.2 = (s32[3072]{0:T(1024)S(1)}, s32[3072]{0:T(1024)}, u32[]{:S(2)}) copy-start(s32[3072]{0:T(1024)} %param.15) | copy-start | bytes 36868
  33.4 92.9 %all-to-all-start = ((f32[64,8,1024]{2,1,0:T(8,128)}), f32[64,8,1024]{2,1,0:T(8,128)}, u32[]{:S(2)}, u32[]{:S(2)}) async-start(f32[64,8,1024]{2,1,0:T(8,128)} %fusion.9.field_ref), calls=%async_computation | async-start | bytes 4194304 | tf_op jit(solution)/shard_map/all_to_all | solution.py:219

commit v2 on v1

v2 whole, which is shorter than its diff:
```python
import functools

import jax
import jax.numpy as jnp
from jax import lax
from jax.experimental import pallas as pl
from jax.experimental.pallas import tpu as pltpu
from jax.sharding import PartitionSpec as P

BLK = 512
NBLK = 6
LANES = 128
TILE = 256
PARTS = 2
EPS = 1e-06
MESH = pl.DeviceIdType.MESH
VMEM = pl.BlockSpec(memory_space=pltpu.VMEM)
SMEM = pl.BlockSpec(memory_space=pltpu.SMEM)


def forecast(u, coef):
    peers = lax.axis_size("state")
    up = [(i, i + 1) for i in range(peers - 1)]
    down = [(j, i) for i, j in up]
    rows = u.shape[1]
    last = jnp.concatenate([u[:, rows - 2 :], coef[None, rows - 2 :]], axis=0)
    first = jnp.concatenate([u[:, :2], coef[None, :2]], axis=0)
    before = lax.ppermute(last, "state", up)
    after = lax.ppermute(first, "state", down)
    current = jnp.concatenate([before[:-1], u, after[:-1]], axis=1)
    field = jnp.concatenate([before[-1], coef, after[-1]], axis=0)
    for _ in range(2):
        center = current[:, 1:-1]
        field = field[1:-1]
        vertical = current[:, 2:] + current[:, :-2]
        sideways = jnp.pad(center[:, :, 1:], ((0, 0), (0, 0), (0, 1))) + jnp.pad(
            center[:, :, :-1], ((0, 0), (0, 0), (1, 0))
        )
        current = center + field * (vertical + sideways - 4.0 * center)
    return current


def pick_kernel(where_ref, lane_ref, field_ref, out_ref):
    members = field_ref.shape[1]
    lane = lax.broadcasted_iota(jnp.int32, (members, LANES), 1)

    def chunk(j, _):
        def step(t, acc):
            for i in range(16):
                k = j * LANES + t * 16 + i
                packed = where_ref[k]
                local = lax.shift_right_logical(packed, 15)
                start = pl.multiple_of(packed & 0x7F80, LANES)
                part = field_ref[local, :, pl.ds(start, LANES)]
                turned = pltpu.roll(part, packed & (LANES - 1), 1)
                acc = jnp.where(lane == lane_ref[k], turned, acc)
            return acc

        acc = lax.fori_loop(0, LANES // 16, step, jnp.zeros((members, LANES), jnp.float32))
        out_ref[:, pl.ds(pl.multiple_of(j * LANES, LANES), LANES)] = acc
        return 0

    lax.fori_loop(0, out_ref.shape[1] // LANES, chunk, 0)


def share_kernel(n_member, n_state, part_ref, out_ref, slots, send_s, recv_s, send_m, recv_m):
    mi = lax.axis_index("member")
    si = lax.axis_index("state")
    barrier = pltpu.get_barrier_semaphore()
    for d in range(1, n_state):
        peer = lax.rem(si + d, n_state)
        pl.semaphore_signal(barrier, inc=1, device_id=(mi, peer), device_id_type=MESH)
    for d in range(1, n_member):
        peer = lax.rem(mi + d, n_member)
        pl.semaphore_signal(barrier, inc=1, device_id=(peer, si), device_id_type=MESH)
    pl.semaphore_wait(barrier, n_state + n_member - 2)
    first = []
    for d in range(1, n_state):
        peer = lax.rem(si + d, n_state)
        copy = pltpu.make_async_remote_copy(
            src_ref=part_ref,
            dst_ref=slots.at[d - 1],
            send_sem=send_s.at[d - 1],
            recv_sem=recv_s.at[d - 1],
            device_id=(mi, peer),
            device_id_type=MESH,
        )
        copy.start()
        first.append(copy)
    total = part_ref[...]
    for d in range(1, n_state):
        first[d - 1].wait()
        total = total + slots[d - 1]
    out_ref[mi] = total
    second = []
    for d in range(1, n_member):
        peer = lax.rem(mi + d, n_member)
        copy = pltpu.make_async_remote_copy(
            src_ref=out_ref.at[mi],
            dst_ref=out_ref.at[mi],
            send_sem=send_m.at[d - 1],
            recv_sem=recv_m.at[d - 1],
            device_id=(peer, si),
            device_id_type=MESH,
        )
        copy.start()
        second.append(copy)
    for copy in second:
        copy.wait()


def anomalies(values):
    return (values - jnp.mean(values, axis=0, keepdims=True)).astype(jnp.bfloat16)


def observed_kernel(y0_ref, pcol_ref, prow_ref, ybt_ref, dy_ref, q_ref, y_ref):
    members = y0_ref.shape[0]
    y_ref[...] = y0_ref[...]

    def block(b, _):
        own = pl.ds(pl.multiple_of(b * BLK, BLK), BLK)
        values = y_ref[:, own]
        mean = jnp.mean(values, axis=0, keepdims=True)
        anomaly = values - mean
        spread = jnp.sum(anomaly * anomaly, axis=0, keepdims=True) / (members - 1) + EPS
        observed = prow_ref[3:4, own]
        variance = prow_ref[4:5, own]
        post = spread * variance / (spread + variance)
        center = post * (mean / spread + observed / variance)
        shrink = jnp.sqrt(variance / (variance + spread)) - 1.0
        dy_ref[:, own] = (center - mean + shrink * anomaly).astype(jnp.bfloat16)
        turned = anomaly.T
        ybt_ref[own, :] = turned.astype(jnp.bfloat16)
        spread_c = jnp.sum(turned * turned, axis=1, keepdims=True) / (members - 1) + EPS
        q = jnp.sqrt(1.0 / (spread_c * (members - 1)))
        reach = pcol_ref[own, 2:3]
        q_ref[own, 0:1] = q
        q_ref[own, 1:2] = q / (reach * reach)

        def later(t, _):
            at = pl.ds(pl.multiple_of(t * TILE, TILE), TILE)
            y = y_ref[:, at]
            cov = jnp.dot(ybt_ref[own, :], anomalies(y), preferred_element_type=jnp.float32)
            gap_r = prow_ref[0:1, at] - pcol_ref[own, 0:1]
            gap_c = prow_ref[1:2, at] - pcol_ref[own, 1:2]
            far = (gap_r * gap_r + gap_c * gap_c) * q_ref[own, 1:2]
            w = jnp.maximum(q_ref[own, 0:1] - far, 0.0)
            gain = (w * w * cov).astype(jnp.bfloat16)
            y_ref[:, at] = y + jnp.dot(dy_ref[:, own], gain, preferred_element_type=jnp.float32)
            return 0

        per = BLK // TILE
        lax.fori_loop((b + 1) * per, NBLK * per, later, 0)
        return 0

    lax.fori_loop(0, NBLK, block, 0)


def cells_kernel(
    first_col, base_ref, x_ref, pcol_ref, ybt_ref, dy_ref, q_ref, out_ref, near_ref, across_ref
):
    rows, members, cols = x_ref.shape
    base = base_ref[0].astype(jnp.float32)
    out_ref[...] = x_ref[...]
    groups = TILE // LANES
    together = 4 if rows % 4 == 0 else 1

    def block(b, _):
        own = pl.ds(pl.multiple_of(b * BLK, BLK), BLK)
        obs_r = pcol_ref[own, 0:1]
        obs_c = pcol_ref[own, 1:2]
        q = q_ref[own, 0:1]
        inv = q_ref[own, 1:2]
        for r in range(rows):
            gap = base + float(r) - obs_r
            near_ref[r] = jnp.broadcast_to(q - gap * gap * inv, (BLK, LANES))

        def column(t, _):
            at = pl.ds(pl.multiple_of(t * TILE, TILE), TILE)
            place = lax.broadcasted_iota(jnp.int32, (1, TILE), 1) + (t * TILE + first_col)
            gap = place.astype(jnp.float32) - obs_c
            across_ref[...] = gap * gap * inv

            def row(g, _):
                xs = [out_ref[g * together + i, :, at] for i in range(together)]
                news = []
                for i in range(together):
                    cov = jnp.dot(
                        ybt_ref[own, :], anomalies(xs[i]), preferred_element_type=jnp.float32
                    )
                    near = jnp.concatenate([near_ref[g * together + i]] * groups, axis=1)
                    w = jnp.maximum(near - across_ref[...], 0.0)
                    gain = (w * w * cov).astype(jnp.bfloat16)
                    news.append(
                        xs[i] + jnp.dot(dy_ref[:, own], gain, preferred_element_type=jnp.float32)
                    )
                for i in range(together):
                    out_ref[g * together + i, :, at] = news[i]
                return 0

            lax.fori_loop(0, rows // together, row, 0)
            return 0

        lax.fori_loop(0, cols // TILE, column, 0)
        return 0

    lax.fori_loop(0, NBLK, block, 0)


def on_device(prior, coef, observations, obs_variance, obs_row, obs_col, obs_radius, block_order):
    n_member = lax.axis_size("member")
    n_state = lax.axis_size("state")
    local_members, local_rows, cols = prior.shape
    members = local_members * n_member
    n_obs = block_order.shape[0]
    f32 = jnp.float32
    table = jnp.stack(
        [
            obs_row.astype(f32),
            obs_col.astype(f32),
            obs_radius.astype(f32),
            observations,
            obs_variance,
        ]
        + [jnp.zeros((n_obs,), f32)] * 3,
        axis=1,
    )
    by_obs = jnp.take(table, block_order, axis=0)
    by_field = by_obs.T
    row_i = by_field[0].astype(jnp.int32)
    col_i = by_field[1].astype(jnp.int32)

    now = forecast(prior, coef).transpose(1, 0, 2)
    base_row = lax.axis_index("state") * local_rows
    tile_rows = local_rows // n_member
    first_row = base_row + lax.axis_index("member") * tile_rows
    width = cols // PARTS
    cells = [
        lax.all_to_all(
            now[:, :, p * width : (p + 1) * width], "member", split_axis=0, concat_axis=1, tiled=True
        )
        for p in range(PARTS)
    ]

    local = row_i - base_row
    inside = (local >= 0) & (local < local_rows)
    index = jnp.arange(n_obs, dtype=jnp.int32)
    turn = (index - col_i) & (LANES - 1)
    packed = (jnp.where(inside, local, 0) << 15) | (col_i & 0x7F80) | turn
    target = jnp.where(inside, index & (LANES - 1), -1)
    part = pl.pallas_call(
        pick_kernel,
        out_shape=jax.ShapeDtypeStruct((local_members, n_obs), f32),
        in_specs=[SMEM, SMEM, VMEM],
        out_specs=VMEM,
        compiler_params=pltpu.CompilerParams(vmem_limit_bytes=32 * 1024 * 1024),
        cost_estimate=pl.CostEstimate(flops=10**7, bytes_accessed=10**7, transcendentals=0),
    )(packed, target, now)
    shared = pl.pallas_call(
        functools.partial(share_kernel, n_member, n_state),
        out_shape=jax.ShapeDtypeStruct((n_member, local_members, n_obs), f32),
        in_specs=[VMEM],
        out_specs=VMEM,
        scratch_shapes=[
            pltpu.VMEM((n_state - 1, local_members, n_obs), f32),
            pltpu.SemaphoreType.DMA((n_state - 1,)),
            pltpu.SemaphoreType.DMA((n_state - 1,)),
            pltpu.SemaphoreType.DMA((n_member - 1,)),
            pltpu.SemaphoreType.DMA((n_member - 1,)),
        ],
        compiler_params=pltpu.CompilerParams(
            collective_id=0, has_side_effects=True, vmem_limit_bytes=32 * 1024 * 1024
        ),
    )(part)
    y0 = shared.reshape(members, n_obs)
    ybt, dy, q = pl.pallas_call(
        observed_kernel,
        out_shape=[
            jax.ShapeDtypeStruct((n_obs, members), jnp.bfloat16),
            jax.ShapeDtypeStruct((members, n_obs), jnp.bfloat16),
            jax.ShapeDtypeStruct((n_obs, 8), f32),
        ],
        in_specs=[VMEM] * 3,
        out_specs=[VMEM] * 3,
        scratch_shapes=[pltpu.VMEM((members, n_obs), f32)],
        compiler_params=pltpu.CompilerParams(vmem_limit_bytes=40 * 1024 * 1024),
        cost_estimate=pl.CostEstimate(flops=10**9, bytes_accessed=10**7, transcendentals=0),
    )(y0, by_obs, by_field)
    backs = []
    for p in range(PARTS):
        result = pl.pallas_call(
            functools.partial(cells_kernel, p * width),
            out_shape=jax.ShapeDtypeStruct(cells[p].shape, f32),
            in_specs=[SMEM] + [VMEM] * 5,
            out_specs=VMEM,
            scratch_shapes=[
                pltpu.VMEM((tile_rows, BLK, LANES), f32),
                pltpu.VMEM((BLK, TILE), f32),
            ],
            compiler_params=pltpu.CompilerParams(vmem_limit_bytes=40 * 1024 * 1024),
            cost_estimate=pl.CostEstimate(
                flops=2 * 10**10, bytes_accessed=10**7, transcendentals=0
            ),
        )(jnp.reshape(first_row, (1,)).astype(jnp.int32), cells[p], by_obs, ybt, dy, q)
        backs.append(
            lax.all_to_all(result, "member", split_axis=1, concat_axis=0, tiled=True)
        )
    return jnp.concatenate([back.transpose(1, 0, 2) for back in backs], axis=2)


def solution(mesh):
    in_specs = (P("member", "state", None), P("state", None), P(), P(), P(), P(), P(), P())
    out_specs = P("member", "state", None)
    return jax.shard_map(
        on_device, mesh=mesh, in_specs=in_specs, out_specs=out_specs, check_vma=False
    )
```

time: 296 us -> 239 us (0.81)
  blocking collectives: 57.1 us -> 0 us
  Pallas kernels: 184 us -> 136 us
  waiting for transfers between devices: 6.19 us -> 25.3 us
  starting transfers between devices: 11.2 us -> 29.8 us
  other arithmetic: 6.66 us -> 14.3 us
    all_to_all x1 -> x0, blocking collectives: 57.1 us -> none  [on_device(): lax.all_to_all(result, 'member', split_axis=1, concat_axis=0, tiled=True)]
    pallas_call x1, Pallas kernels: 54.2 us -> 19.8 us  [on_device(): pl.pallas_call(pick_kernel, out_shape=jax.ShapeDtypeStruct((local_members...]
    all_to_all x1 -> x4, waiting for transfers between devices: 0.01 us -> 25.3 us  [the longest x2 25.3 us: on_device(): lax.all_to_all(result, 'member', split_axis=1, concat_axis=0, tiled=True)]
    all_to_all x1 -> x4, starting transfers between devices: 5.02 us -> 23.6 us  [the longest x2 13.4 us: on_device(): lax.all_to_all(now[:, :, p * width:(p + 1) * width], 'member', split_axis...]
    pallas_call x1 -> x3, Pallas kernels: 106 us -> 90.6 us  [the longest x2 72.4 us: on_device(): pl.pallas_call(functools.partial(cells_kernel, p * width), out_shape=jax....]
    ppermute x2, waiting for transfers between devices: 6.18 us -> 0.01 us  [the longest x1 0.01 us: forecast(): before = lax.ppermute(last, 'state', up)]
    concatenate x1 -> x0, local copies, waits for them, and re-layouts: 6.06 us -> none  [forecast(): both = jnp.concatenate([u, coef[None]], axis=0)]
    select_n x2, other arithmetic: 0.03 us -> 5.16 us  [on_device(): by_obs = jnp.take(table, block_order, axis=0)]
  transfers between devices with their start and end apart: 3 -> 6, of which waited for: 2 -> 1; matrix products, arithmetic and copies ran while one was open for 3% -> 12% of each run, Pallas kernels for 26% -> 57%
where the time goes in v2:
time: 239 us; the launch traced here: 238 us
  Pallas kernels  136 us (57%)
  local copies, waits for them, and re-layouts  32 us (13%)
  starting transfers between devices  29.8 us (12%)
  waiting for transfers between devices  25.3 us (11%)
  other arithmetic  14.3 us (6%)
    pallas_call x2, Pallas kernels, on_device(): pl.pallas_call(functools.partial(cells_kernel, p * width), out_shape=jax....  72.4 us
    pallas_call x1, Pallas kernels, on_device(): pl.pallas_call(functools.partial(share_kernel, n_member, n_state), out_sh...  25.9 us
    all_to_all x2, waiting for transfers between devices, on_device(): lax.all_to_all(result, 'member', split_axis=1, concat_axis=0, tiled=True)  25.3 us
    pallas_call x1, Pallas kernels, on_device(): pl.pallas_call(pick_kernel, out_shape=jax.ShapeDtypeStruct((local_members...  19.8 us
    pallas_call x1, Pallas kernels, on_device(): pl.pallas_call(observed_kernel, out_shape=[jax.ShapeDtypeStruct((n_obs, m...  18.2 us
    all_to_all x2, starting transfers between devices, on_device(): lax.all_to_all(now[:, :, p * width:(p + 1) * width], 'member', split_axis...  13.4 us
    gather x1, local copies, waits for them, and re-layouts, on_device(): by_obs = jnp.take(table, block_order, axis=0)  10.9 us
    all_to_all x2, starting transfers between devices, on_device(): lax.all_to_all(result, 'member', split_axis=1, concat_axis=0, tiled=True)  10.2 us
  transfers between devices with their start and end apart: 6, of which 1 were waited for; matrix products, arithmetic and copies ran while one was open for 12% of the time, Pallas kernels for 57%

profile of v2, /device:TPU:0, one launch (start us, length us, event | category | flops | bytes accessed | tf_op | source)
XLA Modules:
  0.0 238.1 jit_solution(9754749286515320362)
XLA Ops:
  0.0 2.8 %copy.34 = f32[8,64,1024]{2,0,1:T(8,128)S(1)} copy(f32[8,64,1024]{2,1,0:T(8,128)} %param.8) | data formatting | bytes 4194304 | tf_op args[0]
  4.3 4.9 %collective-permute-start = (f32[9,2,1024]{2,0,1:T(8,128)S(1)}, f32[9,2,1024]{2,0,1:T(8,128)S(1)}, u32[]{:S(2)}, u32[]{:S(2)}) collective-permute-start(f32[9,2,1024]{2,0,1:T(8,128)S(1)} %pad_maximum_fusion.4), channel_id=1, source_target_pairs={{0,1},{1,2},{2,3},{4,5},{5,6},{6,7},{8,9},{9,10},{10,11},{12,13},{... | collective-permute-start | bytes 221192 | tf_op jit(solution)/shard_map/ppermute | solution.py:28
  11.3 10.9 %gather_fusion = f32[3072,8]{1,0:T(8,128)} fusion(f32[3072,8]{1,0:T(8,128)S(1)} %copy.40, s32[3072]{0:T(1024)S(1)} %fusion.12), kind=kCustom, calls=%fused_computation | custom fusion | bytes 208896 | tf_op jit(solution)/shard_map/jit(_take)/gather | solution.py:228
  22.2 1.7 pad_maximum_fusion
  28.8 1.5 fusion.15
  30.4 4.9 %all-to-all-start = ((f32[64,8,512]{2,1,0:T(8,128)}), f32[64,8,512]{2,1,0:T(8,128)S(1)}, u32[]{:S(2)}, u32[]{:S(2)}) async-start(f32[64,8,512]{2,1,0:T(8,128)} %get-tuple-element.17), calls=%async_computation | async-start | bytes 2097152 | tf_op jit(solution)/shard_map/all_to_all | solution.py:239
  35.2 3.6 %fusion.18 = f32[8,3072]{0,1:T(8,128)} fusion(f32[3072,8]{1,0:T(8,128)} %gather_fusion, pred[3072]{0:T(1024)(128)(4,1)S(1)} %compare_and_fusion.1), kind=kLoop, calls=%fused_computation.41 | loop fusion | flops 24576 | bytes 199680 | tf_op jit(solution)/shard_map/jit(_take)/select_n | solution.py:228
  38.8 1.8 copy.41.prow_ref
  40.6 3.3 %fusion.11 = (s32[3072]{0:T(1024)S(1)}, s32[3072]{0:T(1024)S(1)}) fusion(f32[8,3072]{0,1:T(8,128)} %fusion.18, s32[]{:T(128)S(6)} %mul.34), kind=kLoop, calls=%fused_computation.18 | loop fusion | flops 9216 | bytes 49156 | tf_op jit(solution)/shard_map/sub | solution.py:245
  44.0 1.6 broadcast_select_fusion.pcol_ref
  45.6 19.8 %shard_map.82.part_ref = f32[8,3072]{1,0:T(8,128)S(1)} custom-call(s32[3072]{0:T(1024)S(1)} %get-tuple-element.24.where_ref, s32[3072]{0:T(1024)S(1)} %get-tuple-element.23.lane_ref, f32[64,8,1024]{2,1,0:T(8,128)S(1)} %fusion.8.field_ref), custom_call_target="tpu_custom_call" | custom-call | flops 10000000 | bytes 10000000 | tf_op jit(solution)/shard_map/pallas_call | solution.py:251
  65.4 25.9 %shard_map.83 = f32[8,8,3072]{2,1,0:T(8,128)S(1)} custom-call(f32[8,3072]{1,0:T(8,128)S(1)} %shard_map.82.part_ref), custom_call_target="tpu_custom_call" | custom-call | tf_op jit(solution)/shard_map/pallas_call | solution.py:259
  91.4 18.2 %shard_map.84 = (bf16[3072,64]{1,0:T(8,128)(2,1)S(1)}, bf16[64,3072]{1,0:T(8,128)(2,1)S(1)}, f32[3072,8]{1,0:T(8,128)S(1)}) custom-call(f32[64,3072]{1,0:T(8,128)S(1)} %bitcast.47, f32[3072,8]{1,0:T(8,128)S(1)} %broadcast_select_fusion.pcol_ref, f32[8,3072]{1,0:T(8,128)S(1)} %copy.41.prow_ref), custom_call_target="tpu_custom_call" | custom-call | flops 1000000000 | bytes 10000000 | tf_op jit(solution)/shard_map/pallas_call | solution.py:276
  112.7 8.5 %all-to-all-start.2 = ((f32[64,8,512]{2,1,0:T(8,128)}), f32[64,8,512]{2,1,0:T(8,128)}, u32[]{:S(2)}, u32[]{:S(2)}) async-start(f32[64,8,512]{2,1,0:T(8,128)} %get-tuple-element.18), calls=%async_computation.2 | async-start | bytes 2097152 | tf_op jit(solution)/shard_map/all_to_all | solution.py:239
  121.3 1.4 copy.58
  122.7 36.2 %shard_map.85 = f32[8,64,512]{2,1,0:T(8,128)S(1)} custom-call(s32[1]{0:T(128)} %bitcast.base_ref, f32[8,64,512]{2,1,0:T(8,128)S(1)} %bitcast.46, f32[3072,8]{1,0:T(8,128)S(1)} %copy-done.1, bf16[3072,64]{1,0:T(8,128)(2,1)S(1)} %copy-done.5, bf16[64,3072]{1,0:T(8,128)(2,1)S(1)} %get-tuple-element.9.dy_ref, f32[3072,8]{1,0:T(8,128)S(1)} %copy-done.3), custom_call_target="tpu_custom_call" | custom-call | flops 20000000000 | bytes 10000000 | tf_op jit(solution)/shard_map/pallas_call | solution.py:291
  158.9 1.6 copy.42
  160.5 5.1 %all-to-all-start.1 = ((f32[8,64,512]{2,0,1:T(8,128)}), f32[8,64,512]{2,0,1:T(8,128)}, u32[]{:S(2)}, u32[]{:S(2)}) async-start(f32[8,64,512]{2,0,1:T(8,128)} %copy.42), calls=%async_computation.1 | async-start | bytes 2097152 | tf_op jit(solution)/shard_map/all_to_all | solution.py:306
  165.6 1.4 copy.56
  167.1 36.2 %shard_map.86 = f32[8,64,512]{2,1,0:T(8,128)S(1)} custom-call(s32[1]{0:T(128)} %bitcast.base_ref, f32[8,64,512]{2,1,0:T(8,128)S(1)} %bitcast.45, f32[3072,8]{1,0:T(8,128)S(1)} %copy-done.1, bf16[3072,64]{1,0:T(8,128)(2,1)S(1)} %copy-done.6, bf16[64,3072]{1,0:T(8,128)(2,1)S(1)} %get-tuple-element.9.dy_ref, f32[3072,8]{1,0:T(8,128)S(1)} %copy-done.3), custom_call_target="tpu_custom_call" | custom-call | flops 20000000000 | bytes 10000000 | tf_op jit(solution)/shard_map/pallas_call | solution.py:291
  203.3 1.6 copy.45
  204.8 5.1 %all-to-all-start.3 = ((f32[8,64,512]{2,0,1:T(8,128)}), f32[8,64,512]{2,0,1:T(8,128)S(1)}, u32[]{:S(2)}, u32[]{:S(2)}) async-start(f32[8,64,512]{2,0,1:T(8,128)} %copy.45), calls=%async_computation.3 | async-start | bytes 2097152 | tf_op jit(solution)/shard_map/all_to_all | solution.py:306
  211.3 25.3 %all-to-all-done.3 = f32[8,64,512]{2,0,1:T(8,128)S(1)} async-done(((f32[8,64,512]{2,0,1:T(8,128)}), f32[8,64,512]{2,0,1:T(8,128)S(1)}, u32[]{:S(2)}, u32[]{:S(2)}) %all-to-all-start.3) | async-done | bytes 1048608 | tf_op jit(solution)/shard_map/all_to_all | solution.py:306
  236.6 1.5 pad_maximum_fusion.1
  (71 shorter events, 12.8 us)
Async XLA Ops:
  0.0 4.2 %copy-start.11 = (f32[64,1024]{1,0:T(8,128)S(1)}, f32[64,1024]{1,0:T(8,128)}, u32[]{:S(2)}) copy-start(f32[64,1024]{1,0:T(8,128)} %param.9) | copy-start | bytes 786436
  0.0 10.5 %copy-start.12 = (s32[3072]{0:T(1024)S(1)}, s32[3072]{0:T(1024)}, u32[]{:S(2)}) copy-start(s32[3072]{0:T(1024)} %param.15) | copy-start | bytes 36868
  0.0 10.5 %copy-start.15 = (s32[3072]{0:T(1024)S(1)}, s32[3072]{0:T(1024)}, u32[]{:S(2)}) copy-start(s32[3072]{0:T(1024)} %param.12) | copy-start | bytes 36868
  0.0 10.5 %copy-start.16 = (s32[3072]{0:T(1024)S(1)}, s32[3072]{0:T(1024)}, u32[]{:S(2)}) copy-start(s32[3072]{0:T(1024)} %param.13) | copy-start | bytes 36868
  0.0 10.6 %copy-start.17 = (s32[3072]{0:T(1024)S(1)}, s32[3072]{0:T(1024)}, u32[]{:S(2)}) copy-start(s32[3072]{0:T(1024)} %param.14) | copy-start | bytes 36868
  0.0 10.6 %copy-start.13 = (f32[3072]{0:T(1024)S(1)}, f32[3072]{0:T(1024)}, u32[]{:S(2)}) copy-start(f32[3072]{0:T(1024)} %param.10) | copy-start | bytes 36868
  0.0 10.6 %copy-start.14 = (f32[3072]{0:T(1024)S(1)}, f32[3072]{0:T(1024)}, u32[]{:S(2)}) copy-start(f32[3072]{0:T(1024)} %param.11) | copy-start | bytes 36868
  2.9 1.3 copy-start.7
  4.3 17.9 %collective-permute-start = (f32[9,2,1024]{2,0,1:T(8,128)S(1)}, f32[9,2,1024]{2,0,1:T(8,128)S(1)}, u32[]{:S(2)}, u32[]{:S(2)}) collective-permute-start(f32[9,2,1024]{2,0,1:T(8,128)S(1)} %pad_maximum_fusion.4), channel_id=1, source_target_pairs={{0,1},{1,2},{2,3},{4,5},{5,6},{6,7},{8,9},{9,10},{10,11},{12,13},{... | collective-permute-start | bytes 221192 | tf_op jit(solution)/shard_map/ppermute | solution.py:28
  9.2 13.0 %collective-permute-start.1 = (f32[9,2,1024]{2,0,1:T(8,128)S(1)}, f32[9,2,1024]{2,0,1:T(8,128)S(1)}, u32[]{:S(2)}, u32[]{:S(2)}) collective-permute-start(f32[9,2,1024]{2,0,1:T(8,128)S(1)} %pad_maximum_fusion.5), channel_id=1, source_target_pairs={{1,0},{2,1},{3,2},{5,4},{6,5},{7,6},{9,8},{10,9},{11,10},{13,12},{... | collective-permute-start | bytes 221192 | tf_op jit(solution)/shard_map/ppermute | solution.py:29
  24.0 1.6 copy-start.8
  30.4 81.4 %all-to-all-start = ((f32[64,8,512]{2,1,0:T(8,128)}), f32[64,8,512]{2,1,0:T(8,128)S(1)}, u32[]{:S(2)}, u32[]{:S(2)}) async-start(f32[64,8,512]{2,1,0:T(8,128)} %get-tuple-element.17), calls=%async_computation | async-start | bytes 2097152 | tf_op jit(solution)/shard_map/all_to_all | solution.py:239
  40.6 3.3 %copy-start.9 = (f32[3072,8]{1,0:T(8,128)S(1)}, f32[3072,8]{1,0:T(8,128)}, u32[]{:S(2)}) copy-start(f32[3072,8]{1,0:T(8,128)} %gather_fusion) | copy-start | bytes 294916
  45.6 45.8 %copy-start = (f32[3072,8]{1,0:T(8,128)}, f32[3072,8]{1,0:T(8,128)S(1)}, u32[]{:S(2)}) copy-start(f32[3072,8]{1,0:T(8,128)S(1)} %broadcast_select_fusion.pcol_ref) | copy-start | bytes 294916
  109.6 1.2 copy-start.2
  110.8 0.9 copy-start.4
  111.7 1.0 copy-start.10
  112.7 9.9 %copy-start.1 = (f32[3072,8]{1,0:T(8,128)S(1)}, f32[3072,8]{1,0:T(8,128)}, u32[]{:S(2)}) copy-start(f32[3072,8]{1,0:T(8,128)} %copy-done) | copy-start | bytes 294916
  112.7 9.9 %copy-start.3 = (f32[3072,8]{1,0:T(8,128)S(1)}, f32[3072,8]{1,0:T(8,128)}, u32[]{:S(2)}) copy-start(f32[3072,8]{1,0:T(8,128)} %copy-done.2) | copy-start | bytes 294916
  112.7 47.8 %all-to-all-start.2 = ((f32[64,8,512]{2,1,0:T(8,128)}), f32[64,8,512]{2,1,0:T(8,128)}, u32[]{:S(2)}, u32[]{:S(2)}) async-start(f32[64,8,512]{2,1,0:T(8,128)} %get-tuple-element.18), calls=%async_computation.2 | async-start | bytes 2097152 | tf_op jit(solution)/shard_map/all_to_all | solution.py:239
  121.3 1.4 copy-start.5
  160.5 44.3 %all-to-all-start.1 = ((f32[8,64,512]{2,0,1:T(8,128)}), f32[8,64,512]{2,0,1:T(8,128)}, u32[]{:S(2)}, u32[]{:S(2)}) async-start(f32[8,64,512]{2,0,1:T(8,128)} %copy.42), calls=%async_computation.1 | async-start | bytes 2097152 | tf_op jit(solution)/shard_map/all_to_all | solution.py:306
  165.6 1.4 copy-start.6
  204.8 31.7 %all-to-all-start.3 = ((f32[8,64,512]{2,0,1:T(8,128)}), f32[8,64,512]{2,0,1:T(8,128)S(1)}, u32[]{:S(2)}, u32[]{:S(2)}) async-start(f32[8,64,512]{2,0,1:T(8,128)} %copy.45), calls=%async_computation.3 | async-start | bytes 2097152 | tf_op jit(solution)/shard_map/all_to_all | solution.py:306

commit v3 on v2

--- a/solution.py
+++ b/solution.py
@@ -157,7 +157,7 @@
 
 
 def cells_kernel(
-    first_col, base_ref, x_ref, pcol_ref, ybt_ref, dy_ref, q_ref, out_ref, near_ref, across_ref
+    n_tiles, first_col, base_ref, span_ref, x_ref, pcol_ref, ybt_ref, dy_ref, q_ref, out_ref, near_ref, across_ref
 ):
     rows, members, cols = x_ref.shape
     base = base_ref[0].astype(jnp.float32)
@@ -168,7 +168,6 @@
     def block(b, _):
         own = pl.ds(pl.multiple_of(b * BLK, BLK), BLK)
         obs_r = pcol_ref[own, 0:1]
-        obs_c = pcol_ref[own, 1:2]
         q = q_ref[own, 0:1]
         inv = q_ref[own, 1:2]
         for r in range(rows):
@@ -178,33 +177,60 @@
         def column(t, _):
             at = pl.ds(pl.multiple_of(t * TILE, TILE), TILE)
             place = lax.broadcasted_iota(jnp.int32, (1, TILE), 1) + (t * TILE + first_col)
-            gap = place.astype(jnp.float32) - obs_c
-            across_ref[...] = gap * gap * inv
-
-            def row(g, _):
-                xs = [out_ref[g * together + i, :, at] for i in range(together)]
-                news = []
-                for i in range(together):
-                    cov = jnp.dot(
-                        ybt_ref[own, :], anomalies(xs[i]), preferred_element_type=jnp.float32
-                    )
-                    near = jnp.concatenate([near_ref[g * together + i]] * groups, axis=1)
-                    w = jnp.maximum(near - across_ref[...], 0.0)
-                    gain = (w * w * cov).astype(jnp.bfloat16)
-                    news.append(
-                        xs[i] + jnp.dot(dy_ref[:, own], gain, preferred_element_type=jnp.float32)
-                    )
-                for i in range(together):
-                    out_ref[g * together + i, :, at] = news[i]
-                return 0
-
-            lax.fori_loop(0, rows // together, row, 0)
+            place = place.astype(jnp.float32)
+            entry = (b * n_tiles + first_col // TILE + t) * 2
+            lead = span_ref[entry] * LANES
+            count = span_ref[entry + 1]
+
+            def window(size):
+                mine = pl.ds(pl.multiple_of(lead, LANES), size)
+                ours = pl.ds(pl.multiple_of(b * BLK + lead, LANES), size)
+                gap = place - pcol_ref[ours, 1:2]
+                across_ref[0:size, :] = gap * gap * q_ref[ours, 1:2]
+
+                def row(g, _):
+                    xs = [out_ref[g * together + i, :, at] for i in range(together)]
+                    news = []
+                    for i in range(together):
+                        cov = jnp.dot(
+                            ybt_ref[ours, :], anomalies(xs[i]), preferred_element_type=jnp.float32
+                        )
+                        near = jnp.concatenate([near_ref[g * together + i, mine, :]] * groups, axis=1)
+                        w = jnp.maximum(near - across_ref[0:size, :], 0.0)
+                        gain = (w * w * cov).astype(jnp.bfloat16)
+                        news.append(
+                            xs[i]
+                            + jnp.dot(dy_ref[:, ours], gain, preferred_element_type=jnp.float32)
+                        )
+                    for i in range(together):
+                        out_ref[g * together + i, :, at] = news[i]
+                    return 0
+
+                lax.fori_loop(0, rows // together, row, 0)
+
+            for parts in range(1, BLK // LANES + 1):
+                pl.when(count == parts)(functools.partial(window, parts * LANES))
             return 0
 
         lax.fori_loop(0, cols // TILE, column, 0)
         return 0
 
     lax.fori_loop(0, NBLK, block, 0)
+
+
+def by_column(table, reach, cols):
+    blocks = table.reshape(NBLK, BLK, table.shape[1])
+    key = blocks[:, :, 1].astype(jnp.int32) * BLK + jnp.arange(BLK, dtype=jnp.int32)
+    rank = jnp.sum((key[:, None, :] < key[:, :, None]).astype(jnp.int32), axis=2)
+    chosen = (jnp.arange(BLK, dtype=jnp.int32)[None, :, None] == rank[:, None, :]).astype(jnp.float32)
+    ordered = jnp.einsum("bpi,bif->bpf", chosen, blocks, precision=lax.Precision.HIGHEST)
+    column = blocks[:, None, :, 1].astype(jnp.int32)
+    start = (jnp.arange(cols // TILE, dtype=jnp.int32) * TILE)[None, :, None]
+    before = jnp.sum((column < start - reach).astype(jnp.int32), axis=2)
+    until = jnp.sum((column < start + TILE + reach).astype(jnp.int32), axis=2)
+    lead = jnp.minimum(before // LANES, BLK // LANES - 1)
+    count = jnp.maximum((until + LANES - 1) // LANES - lead, 0)
+    return ordered.reshape(table.shape), jnp.stack([lead, count], axis=-1).reshape(-1)
 
 
 def on_device(prior, coef, observations, obs_variance, obs_row, obs_col, obs_radius, block_order):
@@ -225,7 +251,7 @@
         + [jnp.zeros((n_obs,), f32)] * 3,
         axis=1,
     )
-    by_obs = jnp.take(table, block_order, axis=0)
+    by_obs, span = by_column(jnp.take(table, block_order, axis=0), jnp.max(obs_radius), cols)
     by_field = by_obs.T
     row_i = by_field[0].astype(jnp.int32)
     col_i = by_field[1].astype(jnp.int32)
@@ -289,9 +315,9 @@
     backs = []
     for p in range(PARTS):
         result = pl.pallas_call(
-            functools.partial(cells_kernel, p * width),
+            functools.partial(cells_kernel, cols // TILE, p * width),
             out_shape=jax.ShapeDtypeStruct(cells[p].shape, f32),
-            in_specs=[SMEM] + [VMEM] * 5,
+            in_specs=[SMEM, SMEM] + [VMEM] * 5,
             out_specs=VMEM,
             scratch_shapes=[
                 pltpu.VMEM((tile_rows, BLK, LANES), f32),
@@ -301,7 +327,7 @@
             cost_estimate=pl.CostEstimate(
                 flops=2 * 10**10, bytes_accessed=10**7, transcendentals=0
             ),
-        )(jnp.reshape(first_row, (1,)).astype(jnp.int32), cells[p], by_obs, ybt, dy, q)
+        )(jnp.reshape(first_row, (1,)).astype(jnp.int32), span, cells[p], by_obs, ybt, dy, q)
         backs.append(
             lax.all_to_all(result, "member", split_axis=1, concat_axis=0, tiled=True)
         )

time: 239 us -> 230 us (0.962)
  Pallas kernels: 136 us -> 127 us
  other arithmetic: 14.3 us -> 10.2 us
  matrix products: 0 us -> 3.97 us
    pallas_call x2, Pallas kernels: 72.4 us -> 62.7 us  [on_device(): pl.pallas_call(functools.partial(cells_kernel, cols // TILE, p * width),...]
    select_n x2 -> x1, other arithmetic: 5.16 us -> 0.02 us  [on_device(): jnp.take(table, block_order, axis=0)]
    dot_general x0 -> x1, matrix products: none -> 3.97 us  [by_column(): jnp.einsum('bpi,bif->bpf', chosen, blocks, precision=lax.Precision.HIGHEST)]
    gather x1 -> x2, local copies, waits for them, and re-layouts: 10.9 us -> 12.9 us  [on_device(): jnp.take(table, block_order, axis=0)]
    unnamed x39 -> x33, local copies, waits for them, and re-layouts: 8.02 us -> 7.06 us
  transfers between devices with their start and end apart: 6 -> 6, of which waited for: 1 -> 1; matrix products, arithmetic and copies ran while one was open for 12% -> 14% of each run, Pallas kernels for 57% -> 55%
where the time goes in v3:
time: 230 us
  Pallas kernels  127 us (55%)
  local copies, waits for them, and re-layouts  33.3 us (14%)
  starting transfers between devices  29.6 us (13%)
  waiting for transfers between devices  25.3 us (11%)
  other arithmetic  10.2 us (4%)
  matrix products  3.97 us (2%)
    pallas_call x2, Pallas kernels, on_device(): pl.pallas_call(functools.partial(cells_kernel, cols // TILE, p * width),...  62.7 us
    pallas_call x1, Pallas kernels, on_device(): pl.pallas_call(functools.partial(share_kernel, n_member, n_state), out_sh...  25.9 us
    all_to_all x2, waiting for transfers between devices, on_device(): lax.all_to_all(result, 'member', split_axis=1, concat_axis=0, tiled=True)  25.3 us
    pallas_call x1, Pallas kernels, on_device(): pl.pallas_call(pick_kernel, out_shape=jax.ShapeDtypeStruct((local_members...  19.8 us
    pallas_call x1, Pallas kernels, on_device(): pl.pallas_call(observed_kernel, out_shape=[jax.ShapeDtypeStruct((n_obs, m...  18.3 us
    all_to_all x2, starting transfers between devices, on_device(): lax.all_to_all(now[:, :, p * width:(p + 1) * width], 'member', split_axis...  13.3 us
    gather x2, local copies, waits for them, and re-layouts, on_device(): jnp.take(table, block_order, axis=0)  12.9 us
    all_to_all x2, starting transfers between devices, on_device(): lax.all_to_all(result, 'member', split_axis=1, concat_axis=0, tiled=True)  10.2 us
  transfers between devices with their start and end apart: 6, of which 1 were waited for; matrix products, arithmetic and copies ran while one was open for 14% of the time, Pallas kernels for 55%

profile of v3, /device:TPU:0, one launch (start us, length us, event | category | flops | bytes accessed | tf_op | source)
XLA Modules:
  0.0 229.7 jit_solution(8888948967012982031)
XLA Ops:
  0.0 2.8 %copy.61 = f32[8,64,1024]{2,0,1:T(8,128)S(1)} copy(f32[8,64,1024]{2,1,0:T(8,128)} %param.8) | data formatting | bytes 4194304 | tf_op args[0]
  4.3 4.9 %collective-permute-start = (f32[9,2,1024]{2,0,1:T(8,128)S(1)}, f32[9,2,1024]{2,0,1:T(8,128)S(1)}, u32[]{:S(2)}, u32[]{:S(2)}) collective-permute-start(f32[9,2,1024]{2,0,1:T(8,128)S(1)} %pad_maximum_fusion.4), channel_id=1, source_target_pairs={{0,1},{1,2},{2,3},{4,5},{5,6},{6,7},{8,9},{9,10},{10,11},{12,13},{... | collective-permute-start | bytes 221192 | tf_op jit(solution)/shard_map/ppermute | solution.py:28
  11.8 10.9 %gather_fusion = f32[3072,8]{1,0:T(8,128)} fusion(f32[3072,8]{1,0:T(8,128)S(1)} %copy.56, s32[3072]{0:T(1024)S(1)} %fusion.14), kind=kCustom, calls=%fused_computation | custom fusion | bytes 208896 | tf_op jit(solution)/shard_map/jit(_take)/gather | solution.py:254
  22.8 2.0 copy.57
  26.1 1.3 fusion.5
  29.3 1.6 fusion.27
  30.8 4.9 %all-to-all-start = ((f32[64,8,512]{2,1,0:T(8,128)}), f32[64,8,512]{2,1,0:T(8,128)}, u32[]{:S(2)}, u32[]{:S(2)}) async-start(f32[64,8,512]{2,1,0:T(8,128)} %get-tuple-element.19), calls=%async_computation | async-start | bytes 2097152 | tf_op jit(solution)/shard_map/all_to_all | solution.py:265
  36.8 4.0 %fusion = f32[6,512,8]{2,1,0:T(8,128)} fusion(f32[6,512,8]{1,2,0:T(8,128)S(1)} %broadcast_select_fusion, s32[6,512]{1,0:T(8,128)S(1)} %convert_reduce_fusion), kind=kOutput, calls=%fused_computation.3 | convolution fusion | flops 152567808 | bytes 208896 | tf_op jit(solution)/shard_map/bpi,bif->bpf/dot_general | solution.py:226
  40.8 1.8 copy.68.prow_ref
  44.0 3.3 %fusion.13 = (s32[3072]{0:T(1024)S(1)}, s32[3072]{0:T(1024)S(1)}) fusion(f32[8,3072]{0,1:T(8,128)} %bitcast.91, s32[]{:T(128)S(6)} %mul.61), kind=kLoop, calls=%fused_computation.22 | loop fusion | flops 9216 | bytes 49156 | tf_op jit(solution)/shard_map/sub | solution.py:271
  47.3 19.8 %shard_map.82.part_ref = f32[8,3072]{1,0:T(8,128)S(1)} custom-call(s32[3072]{0:T(1024)S(1)} %get-tuple-element.26.where_ref, s32[3072]{0:T(1024)S(1)} %get-tuple-element.25.lane_ref, f32[64,8,1024]{2,1,0:T(8,128)S(1)} %fusion.10.field_ref), custom_call_target="tpu_custom_call" | custom-call | flops 10000000 | bytes 10000000 | tf_op jit(solution)/shard_map/pallas_call | solution.py:277
  67.2 25.9 %shard_map.83 = f32[8,8,3072]{2,1,0:T(8,128)S(1)} custom-call(f32[8,3072]{1,0:T(8,128)S(1)} %shard_map.82.part_ref), custom_call_target="tpu_custom_call" | custom-call | tf_op jit(solution)/shard_map/pallas_call | solution.py:285
  93.1 18.3 %shard_map.84 = (bf16[3072,64]{1,0:T(8,128)(2,1)S(1)}, bf16[64,3072]{1,0:T(8,128)(2,1)S(1)}, f32[3072,8]{1,0:T(8,128)S(1)}) custom-call(f32[64,3072]{1,0:T(8,128)S(1)} %bitcast.97, f32[3072,8]{1,0:T(8,128)S(1)} %bitcast.92, f32[8,3072]{1,0:T(8,128)S(1)} %copy.68.prow_ref), custom_call_target="tpu_custom_call" | custom-call | flops 1000000000 | bytes 10000000 | tf_op jit(solution)/shard_map/pallas_call | solution.py:302
  112.6 8.4 %all-to-all-start.2 = ((f32[64,8,512]{2,1,0:T(8,128)}), f32[64,8,512]{2,1,0:T(8,128)}, u32[]{:S(2)}, u32[]{:S(2)}) async-start(f32[64,8,512]{2,1,0:T(8,128)} %get-tuple-element.20), calls=%async_computation.2 | async-start | bytes 2097152 | tf_op jit(solution)/shard_map/all_to_all | solution.py:265
  121.0 1.4 copy.92
  122.7 31.4 %shard_map.85 = f32[8,64,512]{2,1,0:T(8,128)S(1)} custom-call(s32[1]{0:T(128)} %bitcast.base_ref, s32[48]{0:T(128)S(1)} %reshape.182.span_ref, f32[8,64,512]{2,1,0:T(8,128)S(1)} %bitcast.96, f32[3072,8]{1,0:T(8,128)S(1)} %bitcast.93, bf16[3072,64]{1,0:T(8,128)(2,1)S(1)} %get-tuple-element.8.ybt_ref, bf16[64,3072]{1,0:T(8,128)(2,1)S(1)} %get-tuple-element.9.dy_ref, ...), custom_call_target="tpu_custom_call" | custom-call | flops 20000000000 | bytes 10000000 | tf_op jit(solution)/shard_map/pallas_call | solution.py:317
  154.1 1.6 copy.69
  155.7 5.1 %all-to-all-start.1 = ((f32[8,64,512]{2,0,1:T(8,128)}), f32[8,64,512]{2,0,1:T(8,128)}, u32[]{:S(2)}, u32[]{:S(2)}) async-start(f32[8,64,512]{2,0,1:T(8,128)} %copy.69), calls=%async_computation.1 | async-start | bytes 2097152 | tf_op jit(solution)/shard_map/all_to_all | solution.py:332
  162.1 1.4 copy-done.4
  163.5 31.3 %shard_map.86 = f32[8,64,512]{2,1,0:T(8,128)S(1)} custom-call(s32[1]{0:T(128)} %bitcast.base_ref, s32[48]{0:T(128)S(1)} %reshape.182.span_ref, f32[8,64,512]{2,1,0:T(8,128)S(1)} %bitcast.95, f32[3072,8]{1,0:T(8,128)S(1)} %bitcast.94, bf16[3072,64]{1,0:T(8,128)(2,1)S(1)} %get-tuple-element.8.ybt_ref, bf16[64,3072]{1,0:T(8,128)(2,1)S(1)} %get-tuple-element.9.dy_ref, ...), custom_call_target="tpu_custom_call" | custom-call | flops 20000000000 | bytes 10000000 | tf_op jit(solution)/shard_map/pallas_call | solution.py:317
  194.9 1.6 copy.72
  196.4 5.1 %all-to-all-start.3 = ((f32[8,64,512]{2,0,1:T(8,128)}), f32[8,64,512]{2,0,1:T(8,128)S(1)}, u32[]{:S(2)}, u32[]{:S(2)}) async-start(f32[8,64,512]{2,0,1:T(8,128)} %copy.72), calls=%async_computation.3 | async-start | bytes 2097152 | tf_op jit(solution)/shard_map/all_to_all | solution.py:332
  202.9 25.3 %all-to-all-done.3 = f32[8,64,512]{2,0,1:T(8,128)S(1)} async-done(((f32[8,64,512]{2,0,1:T(8,128)}), f32[8,64,512]{2,0,1:T(8,128)S(1)}, u32[]{:S(2)}, u32[]{:S(2)}) %all-to-all-start.3) | async-done | bytes 1048608 | tf_op jit(solution)/shard_map/all_to_all | solution.py:332
  228.2 1.5 pad_maximum_fusion.1
  (80 shorter events, 13.6 us)
Async XLA Ops:
  0.0 4.2 %copy-start.7 = (f32[64,1024]{1,0:T(8,128)S(1)}, f32[64,1024]{1,0:T(8,128)}, u32[]{:S(2)}) copy-start(f32[64,1024]{1,0:T(8,128)} %param.9) | copy-start | bytes 786436
  0.0 10.5 %copy-start.8 = (s32[3072]{0:T(1024)S(1)}, s32[3072]{0:T(1024)}, u32[]{:S(2)}) copy-start(s32[3072]{0:T(1024)} %param.15) | copy-start | bytes 36868
  0.0 10.5 %copy-start.11 = (s32[3072]{0:T(1024)S(1)}, s32[3072]{0:T(1024)}, u32[]{:S(2)}) copy-start(s32[3072]{0:T(1024)} %param.14) | copy-start | bytes 36868
  0.0 11.2 %copy-start.12 = (s32[3072]{0:T(1024)S(1)}, s32[3072]{0:T(1024)}, u32[]{:S(2)}) copy-start(s32[3072]{0:T(1024)} %param.12) | copy-start | bytes 36868
  0.0 11.2 %copy-start.13 = (s32[3072]{0:T(1024)S(1)}, s32[3072]{0:T(1024)}, u32[]{:S(2)}) copy-start(s32[3072]{0:T(1024)} %param.13) | copy-start | bytes 36868
  0.0 11.2 %copy-start.9 = (f32[3072]{0:T(1024)S(1)}, f32[3072]{0:T(1024)}, u32[]{:S(2)}) copy-start(f32[3072]{0:T(1024)} %param.10) | copy-start | bytes 36868
  0.0 11.2 %copy-start.10 = (f32[3072]{0:T(1024)S(1)}, f32[3072]{0:T(1024)}, u32[]{:S(2)}) copy-start(f32[3072]{0:T(1024)} %param.11) | copy-start | bytes 36868
  2.9 1.3 copy-start.5
  4.3 20.6 %collective-permute-start = (f32[9,2,1024]{2,0,1:T(8,128)S(1)}, f32[9,2,1024]{2,0,1:T(8,128)S(1)}, u32[]{:S(2)}, u32[]{:S(2)}) collective-permute-start(f32[9,2,1024]{2,0,1:T(8,128)S(1)} %pad_maximum_fusion.4), channel_id=1, source_target_pairs={{0,1},{1,2},{2,3},{4,5},{5,6},{6,7},{8,9},{9,10},{10,11},{12,13},{... | collective-permute-start | bytes 221192 | tf_op jit(solution)/shard_map/ppermute | solution.py:28
  9.2 15.7 %collective-permute-start.1 = (f32[9,2,1024]{2,0,1:T(8,128)S(1)}, f32[9,2,1024]{2,0,1:T(8,128)S(1)}, u32[]{:S(2)}, u32[]{:S(2)}) collective-permute-start(f32[9,2,1024]{2,0,1:T(8,128)S(1)} %pad_maximum_fusion.5), channel_id=1, source_target_pairs={{1,0},{2,1},{3,2},{5,4},{6,5},{7,6},{9,8},{10,9},{11,10},{13,12},{... | collective-permute-start | bytes 221192 | tf_op jit(solution)/shard_map/ppermute | solution.py:29
  22.8 2.1 copy-start.6
  30.8 81.8 %all-to-all-start = ((f32[64,8,512]{2,1,0:T(8,128)}), f32[64,8,512]{2,1,0:T(8,128)}, u32[]{:S(2)}, u32[]{:S(2)}) async-start(f32[64,8,512]{2,1,0:T(8,128)} %get-tuple-element.19), calls=%async_computation | async-start | bytes 2097152 | tf_op jit(solution)/shard_map/all_to_all | solution.py:265
  47.3 45.8 %copy-start = (f32[6,512,8]{2,1,0:T(8,128)S(1)}, f32[6,512,8]{2,1,0:T(8,128)}, u32[]{:S(2)}) copy-start(f32[6,512,8]{2,1,0:T(8,128)} %fusion) | copy-start | bytes 294916
  111.4 1.2 copy-start.2
  112.6 9.8 %copy-start.1 = (f32[6,512,8]{2,1,0:T(8,128)S(1)}, f32[6,512,8]{2,1,0:T(8,128)}, u32[]{:S(2)}) copy-start(f32[6,512,8]{2,1,0:T(8,128)} %fusion) | copy-start | bytes 294916
  112.6 43.1 %all-to-all-start.2 = ((f32[64,8,512]{2,1,0:T(8,128)}), f32[64,8,512]{2,1,0:T(8,128)}, u32[]{:S(2)}, u32[]{:S(2)}) async-start(f32[64,8,512]{2,1,0:T(8,128)} %get-tuple-element.20), calls=%async_computation.2 | async-start | bytes 2097152 | tf_op jit(solution)/shard_map/all_to_all | solution.py:265
  121.0 1.7 copy-start.3
  155.7 40.8 %all-to-all-start.1 = ((f32[8,64,512]{2,0,1:T(8,128)}), f32[8,64,512]{2,0,1:T(8,128)}, u32[]{:S(2)}, u32[]{:S(2)}) async-start(f32[8,64,512]{2,0,1:T(8,128)} %copy.69), calls=%async_computation.1 | async-start | bytes 2097152 | tf_op jit(solution)/shard_map/all_to_all | solution.py:332
  162.1 1.4 copy-start.4
  196.4 31.7 %all-to-all-start.3 = ((f32[8,64,512]{2,0,1:T(8,128)}), f32[8,64,512]{2,0,1:T(8,128)S(1)}, u32[]{:S(2)}, u32[]{:S(2)}) async-start(f32[8,64,512]{2,0,1:T(8,128)} %copy.72), calls=%async_computation.3 | async-start | bytes 2097152 | tf_op jit(solution)/shard_map/all_to_all | solution.py:332

commit v4 on v3

--- a/solution.py
+++ b/solution.py
@@ -63,49 +63,58 @@
     lax.fori_loop(0, out_ref.shape[1] // LANES, chunk, 0)
 
 
-def share_kernel(n_member, n_state, part_ref, out_ref, slots, send_s, recv_s, send_m, recv_m):
+def share_kernel(
+    n_z, n_state, part_ref, out_ref, slots, send_1, recv_1, send_2, recv_2, send_3, recv_3, send_4, recv_4
+):
     mi = lax.axis_index("member")
     si = lax.axis_index("state")
+    core = lax.rem(mi, 2)
+    z = lax.div(mi, 2)
+    sibling = (z * 2 + 1 - core, si)
+    across = [(mi, lax.rem(si + d, n_state)) for d in range(1, n_state)]
+    along = [(lax.rem(z + d, n_z) * 2 + core, si) for d in range(1, n_z)]
     barrier = pltpu.get_barrier_semaphore()
-    for d in range(1, n_state):
-        peer = lax.rem(si + d, n_state)
-        pl.semaphore_signal(barrier, inc=1, device_id=(mi, peer), device_id_type=MESH)
-    for d in range(1, n_member):
-        peer = lax.rem(mi + d, n_member)
-        pl.semaphore_signal(barrier, inc=1, device_id=(peer, si), device_id_type=MESH)
-    pl.semaphore_wait(barrier, n_state + n_member - 2)
-    first = []
-    for d in range(1, n_state):
-        peer = lax.rem(si + d, n_state)
+    for peer in across + along + [sibling]:
+        pl.semaphore_signal(barrier, inc=1, device_id=peer, device_id_type=MESH)
+    pl.semaphore_wait(barrier, n_state + n_z - 1)
+
+    def send(source, target, send_sem, recv_sem, peer):
         copy = pltpu.make_async_remote_copy(
-            src_ref=part_ref,
-            dst_ref=slots.at[d - 1],
-            send_sem=send_s.at[d - 1],
-            recv_sem=recv_s.at[d - 1],
-            device_id=(mi, peer),
+            src_ref=source,
+            dst_ref=target,
+            send_sem=send_sem,
+            recv_sem=recv_sem,
+            device_id=peer,
             device_id_type=MESH,
         )
         copy.start()
-        first.append(copy)
-    total = part_ref[...]
+        return copy
+
+    first = [
+        send(part_ref.at[peer[1]], slots.at[d], send_1.at[d], recv_1.at[d], peer)
+        for d, peer in enumerate(across)
+    ]
+    total = part_ref[si]
+    for d in range(n_state - 1):
+        first[d].wait()
+        total = total + slots[d]
+    out_ref[core, si, z] = total
+    mine = out_ref.at[core, si, z]
+    second = [
+        send(mine, mine, send_2.at[d], recv_2.at[d], peer) for d, peer in enumerate(along)
+    ]
+    for copy in second:
+        copy.wait()
+    line = out_ref.at[core, si]
+    third = [
+        send(line, line, send_3.at[d], recv_3.at[d], peer) for d, peer in enumerate(across)
+    ]
+    last = [send(line, line, send_4.at[0], recv_4.at[0], sibling)]
     for d in range(1, n_state):
-        first[d - 1].wait()
-        total = total + slots[d - 1]
-    out_ref[mi] = total
-    second = []
-    for d in range(1, n_member):
-        peer = lax.rem(mi + d, n_member)
-        copy = pltpu.make_async_remote_copy(
-            src_ref=out_ref.at[mi],
-            dst_ref=out_ref.at[mi],
-            send_sem=send_m.at[d - 1],
-            recv_sem=recv_m.at[d - 1],
-            device_id=(peer, si),
-            device_id_type=MESH,
-        )
-        copy.start()
-        second.append(copy)
-    for copy in second:
+        third[d - 1].wait()
+        other = out_ref.at[core, lax.rem(si + n_state - d, n_state)]
+        last.append(send(other, other, send_4.at[d], recv_4.at[d], sibling))
+    for copy in last:
         copy.wait()
 
 
@@ -190,20 +199,23 @@
 
                 def row(g, _):
                     xs = [out_ref[g * together + i, :, at] for i in range(together)]
-                    news = []
+                    x = jnp.concatenate(xs, axis=1)
+                    cov = jnp.dot(ybt_ref[ours, :], anomalies(x), preferred_element_type=jnp.float32)
+                    far = across_ref[0:size, :]
+                    gains = []
                     for i in range(together):
-                        cov = jnp.dot(
-                            ybt_ref[ours, :], anomalies(xs[i]), preferred_element_type=jnp.float32
+                        near = jnp.concatenate([near_ref[g * together + i, mine, :]] * groups, axis=1)
+                        w = jnp.maximum(near - far, 0.0)
+                        gains.append(
+                            (w * w * cov[:, i * TILE : (i + 1) * TILE]).astype(jnp.bfloat16)
                         )
-                        near = jnp.concatenate([near_ref[g * together + i, mine, :]] * groups, axis=1)
-                        w = jnp.maximum(near - across_ref[0:size, :], 0.0)
-                        gain = (w * w * cov).astype(jnp.bfloat16)
-                        news.append(
-                            xs[i]
-                            + jnp.dot(dy_ref[:, ours], gain, preferred_element_type=jnp.float32)
-                        )
+                    x = x + jnp.dot(
+                        dy_ref[:, ours],
+                        jnp.concatenate(gains, axis=1),
+                        preferred_element_type=jnp.float32,
+                    )
                     for i in range(together):
-                        out_ref[g * together + i, :, at] = news[i]
+                        out_ref[g * together + i, :, at] = x[:, i * TILE : (i + 1) * TILE]
                     return 0
 
                 lax.fori_loop(0, rows // together, row, 0)
@@ -282,23 +294,30 @@
         compiler_params=pltpu.CompilerParams(vmem_limit_bytes=32 * 1024 * 1024),
         cost_estimate=pl.CostEstimate(flops=10**7, bytes_accessed=10**7, transcendentals=0),
     )(packed, target, now)
+    n_z = n_member // 2
+    share = n_obs // n_state
+    dma = pltpu.SemaphoreType.DMA
     shared = pl.pallas_call(
-        functools.partial(share_kernel, n_member, n_state),
-        out_shape=jax.ShapeDtypeStruct((n_member, local_members, n_obs), f32),
+        functools.partial(share_kernel, n_z, n_state),
+        out_shape=jax.ShapeDtypeStruct((2, n_state, n_z, local_members, share), f32),
         in_specs=[VMEM],
         out_specs=VMEM,
         scratch_shapes=[
-            pltpu.VMEM((n_state - 1, local_members, n_obs), f32),
-            pltpu.SemaphoreType.DMA((n_state - 1,)),
-            pltpu.SemaphoreType.DMA((n_state - 1,)),
-            pltpu.SemaphoreType.DMA((n_member - 1,)),
-            pltpu.SemaphoreType.DMA((n_member - 1,)),
+            pltpu.VMEM((n_state - 1, local_members, share), f32),
+            dma((n_state - 1,)),
+            dma((n_state - 1,)),
+            dma((n_z - 1,)),
+            dma((n_z - 1,)),
+            dma((n_state - 1,)),
+            dma((n_state - 1,)),
+            dma((n_state,)),
+            dma((n_state,)),
         ],
         compiler_params=pltpu.CompilerParams(
             collective_id=0, has_side_effects=True, vmem_limit_bytes=32 * 1024 * 1024
         ),
-    )(part)
-    y0 = shared.reshape(members, n_obs)
+    )(part.reshape(local_members, n_state, share).transpose(1, 0, 2))
+    y0 = shared.transpose(2, 0, 3, 1, 4).reshape(members, n_obs)
     ybt, dy, q = pl.pallas_call(
         observed_kernel,
         out_shape=[

time: 230 us -> 200 us (0.87)
  Pallas kernels: 127 us -> 93.5 us
  waiting for transfers between devices: 25.3 us -> 34.3 us
  starting transfers between devices: 29.6 us -> 23.5 us
    pallas_call x2, Pallas kernels: 62.7 us -> 36.4 us  [on_device(): pl.pallas_call(functools.partial(cells_kernel, cols // TILE, p * width),...]
    pallas_call x1, Pallas kernels: 25.9 us -> 18.9 us  [on_device(): pl.pallas_call(functools.partial(share_kernel, n_z, n_state), out_shape=j...]
    all_to_all x2, waiting for transfers between devices: 0.01 us -> 5.18 us  [on_device(): lax.all_to_all(now[:, :, p * width:(p + 1) * width], 'member', split_axis...]
    all_to_all x2, starting transfers between devices: 13.3 us -> 9.35 us  [on_device(): lax.all_to_all(now[:, :, p * width:(p + 1) * width], 'member', split_axis...]
    all_to_all x2, waiting for transfers between devices: 25.3 us -> 29.1 us  [on_device(): lax.all_to_all(result, 'member', split_axis=1, concat_axis=0, tiled=True)]
  transfers between devices with their start and end apart: 6 -> 6, of which waited for: 1 -> 3; matrix products, arithmetic and copies ran while one was open for 14% -> 17% of each run, Pallas kernels for 55% -> 47%
where the time goes in v4:
time: 200 us; the launch traced here: 199 us
  Pallas kernels  93.5 us (47%)
  waiting for transfers between devices  34.3 us (17%)
  local copies, waits for them, and re-layouts  33.4 us (17%)
  starting transfers between devices  23.5 us (12%)
  other arithmetic  10.2 us (5%)
  matrix products  3.97 us (2%)
    pallas_call x2, Pallas kernels, on_device(): pl.pallas_call(functools.partial(cells_kernel, cols // TILE, p * width),...  36.4 us
    all_to_all x2, waiting for transfers between devices, on_device(): lax.all_to_all(result, 'member', split_axis=1, concat_axis=0, tiled=True)  29.1 us
    pallas_call x1, Pallas kernels, on_device(): pl.pallas_call(pick_kernel, out_shape=jax.ShapeDtypeStruct((local_members...  19.8 us
    pallas_call x1, Pallas kernels, on_device(): pl.pallas_call(functools.partial(share_kernel, n_z, n_state), out_shape=j...  18.9 us
    pallas_call x1, Pallas kernels, on_device(): pl.pallas_call(observed_kernel, out_shape=[jax.ShapeDtypeStruct((n_obs, m...  18.3 us
    gather x2, local copies, waits for them, and re-layouts, on_device(): jnp.take(table, block_order, axis=0)  12.9 us
    all_to_all x2, starting transfers between devices, on_device(): lax.all_to_all(now[:, :, p * width:(p + 1) * width], 'member', split_axis...  9.35 us
    all_to_all x2, starting transfers between devices, on_device(): lax.all_to_all(result, 'member', split_axis=1, concat_axis=0, tiled=True)  8.03 us
  transfers between devices with their start and end apart: 6, of which 3 were waited for; matrix products, arithmetic and copies ran while one was open for 17% of the time, Pallas kernels for 47%

profile of v4, /device:TPU:0, one launch (start us, length us, event | category | flops | bytes accessed | tf_op | source)
XLA Modules:
  0.0 199.3 jit_solution(16401737247961551253)
XLA Ops:
  0.0 2.8 %copy.64 = f32[8,64,1024]{2,0,1:T(8,128)S(1)} copy(f32[8,64,1024]{2,1,0:T(8,128)} %param.8) | data formatting | bytes 4194304 | tf_op args[0]
  4.3 4.9 %collective-permute-start = (f32[9,2,1024]{2,0,1:T(8,128)S(1)}, f32[9,2,1024]{2,0,1:T(8,128)S(1)}, u32[]{:S(2)}, u32[]{:S(2)}) collective-permute-start(f32[9,2,1024]{2,0,1:T(8,128)S(1)} %pad_maximum_fusion.4), channel_id=1, source_target_pairs={{0,1},{1,2},{2,3},{4,5},{5,6},{6,7},{8,9},{9,10},{10,11},{12,13},{... | collective-permute-start | bytes 221192 | tf_op jit(solution)/shard_map/ppermute | solution.py:28
  11.8 10.9 %gather_fusion = f32[3072,8]{1,0:T(8,128)} fusion(f32[3072,8]{1,0:T(8,128)S(1)} %copy.59, s32[3072]{0:T(1024)S(1)} %fusion.14), kind=kCustom, calls=%fused_computation | custom fusion | bytes 208896 | tf_op jit(solution)/shard_map/jit(_take)/gather | solution.py:266
  22.8 2.0 copy.60
  29.3 1.6 fusion.27
  30.8 4.9 %all-to-all-start = ((f32[64,8,512]{2,1,0:T(8,128)}), f32[64,8,512]{2,1,0:T(8,128)}, u32[]{:S(2)}, u32[]{:S(2)}) async-start(f32[64,8,512]{2,1,0:T(8,128)} %get-tuple-element.19), calls=%async_computation | async-start | bytes 2097152 | tf_op jit(solution)/shard_map/all_to_all | solution.py:277
  36.8 4.0 %fusion = f32[6,512,8]{2,1,0:T(8,128)} fusion(f32[6,512,8]{1,2,0:T(8,128)S(1)} %broadcast_select_fusion, s32[6,512]{1,0:T(8,128)S(1)} %convert_reduce_fusion), kind=kOutput, calls=%fused_computation.3 | convolution fusion | flops 152567808 | bytes 208896 | tf_op jit(solution)/shard_map/bpi,bif->bpf/dot_general | solution.py:238
  40.8 1.8 copy.72.prow_ref
  44.0 3.3 %fusion.13 = (s32[3072]{0:T(1024)S(1)}, s32[3072]{0:T(1024)S(1)}) fusion(f32[8,3072]{0,1:T(8,128)} %bitcast.95, s32[]{:T(128)S(6)} %mul.61), kind=kLoop, calls=%fused_computation.22 | loop fusion | flops 9216 | bytes 49156 | tf_op jit(solution)/shard_map/sub | solution.py:283
  47.3 19.8 %shard_map.82 = f32[8,3072]{1,0:T(8,128)S(1)} custom-call(s32[3072]{0:T(1024)S(1)} %get-tuple-element.26.where_ref, s32[3072]{0:T(1024)S(1)} %get-tuple-element.25.lane_ref, f32[64,8,1024]{2,1,0:T(8,128)S(1)} %fusion.10.field_ref), custom_call_target="tpu_custom_call" | custom-call | flops 10000000 | bytes 10000000 | tf_op jit(solution)/shard_map/pallas_call | solution.py:289
  67.2 18.9 %shard_map.83 = f32[2,4,4,8,768]{4,3,2,1,0:T(8,128)S(1)} custom-call(f32[4,8,768]{2,1,0:T(8,128)S(1)} %bitcast.103), custom_call_target="tpu_custom_call" | custom-call | tf_op jit(solution)/shard_map/pallas_call | solution.py:300
  86.2 18.3 %shard_map.84 = (bf16[3072,64]{1,0:T(8,128)(2,1)S(1)}, bf16[64,3072]{1,0:T(8,128)(2,1)S(1)}, f32[3072,8]{1,0:T(8,128)S(1)}) custom-call(f32[64,3072]{1,0:T(8,128)S(1)} %bitcast.102, f32[3072,8]{1,0:T(8,128)S(1)} %bitcast.96, f32[8,3072]{1,0:T(8,128)S(1)} %copy.72.prow_ref), custom_call_target="tpu_custom_call" | custom-call | flops 1000000000 | bytes 10000000 | tf_op jit(solution)/shard_map/pallas_call | solution.py:321
  105.7 4.5 %all-to-all-start.2 = ((f32[64,8,512]{2,1,0:T(8,128)}), f32[64,8,512]{2,1,0:T(8,128)}, u32[]{:S(2)}, u32[]{:S(2)}) async-start(f32[64,8,512]{2,1,0:T(8,128)} %get-tuple-element.20), calls=%async_computation.2 | async-start | bytes 2097152 | tf_op jit(solution)/shard_map/all_to_all | solution.py:277
  110.1 1.4 copy.96
  111.9 18.2 %shard_map.85 = f32[8,64,512]{2,1,0:T(8,128)S(1)} custom-call(s32[1]{0:T(128)} %bitcast.base_ref, s32[48]{0:T(128)S(1)} %reshape.185.span_ref, f32[8,64,512]{2,1,0:T(8,128)S(1)} %bitcast.101, f32[3072,8]{1,0:T(8,128)S(1)} %bitcast.97, bf16[3072,64]{1,0:T(8,128)(2,1)S(1)} %get-tuple-element.8.ybt_ref, bf16[64,3072]{1,0:T(8,128)(2,1)S(1)} %get-tuple-element.9.dy_ref, ...), custom_call_target="tpu_custom_call" | custom-call | flops 20000000000 | bytes 10000000 | tf_op jit(solution)/shard_map/pallas_call | solution.py:336
  130.1 1.6 copy.73
  131.7 5.2 %all-to-all-done.2 = f32[64,8,512]{2,1,0:T(8,128)} async-done(((f32[64,8,512]{2,1,0:T(8,128)}), f32[64,8,512]{2,1,0:T(8,128)}, u32[]{:S(2)}, u32[]{:S(2)}) %all-to-all-start.2) | async-done | bytes 1048608 | tf_op jit(solution)/shard_map/all_to_all | solution.py:277
  136.8 4.5 %all-to-all-start.1 = ((f32[8,64,512]{2,0,1:T(8,128)}), f32[8,64,512]{2,0,1:T(8,128)}, u32[]{:S(2)}, u32[]{:S(2)}) async-start(f32[8,64,512]{2,0,1:T(8,128)} %copy.73), calls=%async_computation.1 | async-start | bytes 2097152 | tf_op jit(solution)/shard_map/all_to_all | solution.py:351
  144.0 18.2 %shard_map.86 = f32[8,64,512]{2,1,0:T(8,128)S(1)} custom-call(s32[1]{0:T(128)} %bitcast.base_ref, s32[48]{0:T(128)S(1)} %reshape.185.span_ref, f32[8,64,512]{2,1,0:T(8,128)S(1)} %bitcast.100, f32[3072,8]{1,0:T(8,128)S(1)} %bitcast.98, bf16[3072,64]{1,0:T(8,128)(2,1)S(1)} %get-tuple-element.8.ybt_ref, bf16[64,3072]{1,0:T(8,128)(2,1)S(1)} %get-tuple-element.9.dy_ref, ...), custom_call_target="tpu_custom_call" | custom-call | flops 20000000000 | bytes 10000000 | tf_op jit(solution)/shard_map/pallas_call | solution.py:336
  162.2 1.6 copy.76
  163.8 3.9 %all-to-all-done.1 = f32[8,64,512]{2,0,1:T(8,128)} async-done(((f32[8,64,512]{2,0,1:T(8,128)}), f32[8,64,512]{2,0,1:T(8,128)}, u32[]{:S(2)}, u32[]{:S(2)}) %all-to-all-start.1) | async-done | bytes 1048608 | tf_op jit(solution)/shard_map/all_to_all | solution.py:351
  167.7 3.6 %all-to-all-start.3 = ((f32[8,64,512]{2,0,1:T(8,128)}), f32[8,64,512]{2,0,1:T(8,128)S(1)}, u32[]{:S(2)}, u32[]{:S(2)}) async-start(f32[8,64,512]{2,0,1:T(8,128)} %copy.76), calls=%async_computation.3 | async-start | bytes 2097152 | tf_op jit(solution)/shard_map/all_to_all | solution.py:351
  172.6 25.2 %all-to-all-done.3 = f32[8,64,512]{2,0,1:T(8,128)S(1)} async-done(((f32[8,64,512]{2,0,1:T(8,128)}), f32[8,64,512]{2,0,1:T(8,128)S(1)}, u32[]{:S(2)}, u32[]{:S(2)}) %all-to-all-start.3) | async-done | bytes 1048608 | tf_op jit(solution)/shard_map/all_to_all | solution.py:351
  197.8 1.5 pad_maximum_fusion.1
  (81 shorter events, 16.4 us)
Async XLA Ops:
  0.0 4.2 %copy-start.7 = (f32[64,1024]{1,0:T(8,128)S(1)}, f32[64,1024]{1,0:T(8,128)}, u32[]{:S(2)}) copy-start(f32[64,1024]{1,0:T(8,128)} %param.9) | copy-start | bytes 786436
  0.0 10.5 %copy-start.8 = (s32[3072]{0:T(1024)S(1)}, s32[3072]{0:T(1024)}, u32[]{:S(2)}) copy-start(s32[3072]{0:T(1024)} %param.15) | copy-start | bytes 36868
  0.0 10.5 %copy-start.11 = (s32[3072]{0:T(1024)S(1)}, s32[3072]{0:T(1024)}, u32[]{:S(2)}) copy-start(s32[3072]{0:T(1024)} %param.14) | copy-start | bytes 36868
  0.0 11.2 %copy-start.12 = (s32[3072]{0:T(1024)S(1)}, s32[3072]{0:T(1024)}, u32[]{:S(2)}) copy-start(s32[3072]{0:T(1024)} %param.12) | copy-start | bytes 36868
  0.0 11.2 %copy-start.13 = (s32[3072]{0:T(1024)S(1)}, s32[3072]{0:T(1024)}, u32[]{:S(2)}) copy-start(s32[3072]{0:T(1024)} %param.13) | copy-start | bytes 36868
  0.0 11.2 %copy-start.9 = (f32[3072]{0:T(1024)S(1)}, f32[3072]{0:T(1024)}, u32[]{:S(2)}) copy-start(f32[3072]{0:T(1024)} %param.10) | copy-start | bytes 36868
  0.0 11.2 %copy-start.10 = (f32[3072]{0:T(1024)S(1)}, f32[3072]{0:T(1024)}, u32[]{:S(2)}) copy-start(f32[3072]{0:T(1024)} %param.11) | copy-start | bytes 36868
  2.9 1.3 copy-start.5
  4.3 20.6 %collective-permute-start = (f32[9,2,1024]{2,0,1:T(8,128)S(1)}, f32[9,2,1024]{2,0,1:T(8,128)S(1)}, u32[]{:S(2)}, u32[]{:S(2)}) collective-permute-start(f32[9,2,1024]{2,0,1:T(8,128)S(1)} %pad_maximum_fusion.4), channel_id=1, source_target_pairs={{0,1},{1,2},{2,3},{4,5},{5,6},{6,7},{8,9},{9,10},{10,11},{12,13},{... | collective-permute-start | bytes 221192 | tf_op jit(solution)/shard_map/ppermute | solution.py:28
  9.2 15.7 %collective-permute-start.1 = (f32[9,2,1024]{2,0,1:T(8,128)S(1)}, f32[9,2,1024]{2,0,1:T(8,128)S(1)}, u32[]{:S(2)}, u32[]{:S(2)}) collective-permute-start(f32[9,2,1024]{2,0,1:T(8,128)S(1)} %pad_maximum_fusion.5), channel_id=1, source_target_pairs={{1,0},{2,1},{3,2},{5,4},{6,5},{7,6},{9,8},{10,9},{11,10},{13,12},{... | collective-permute-start | bytes 221192 | tf_op jit(solution)/shard_map/ppermute | solution.py:29
  22.8 2.1 %copy-start.6 = (f32[8,64,1024]{2,0,1:T(8,128)S(1)}, f32[8,64,1024]{2,0,1:T(8,128)}, u32[]{:S(2)}) copy-start(f32[8,64,1024]{2,0,1:T(8,128)} %copy-done.5) | copy-start | bytes 6291460
  30.8 74.8 %all-to-all-start = ((f32[64,8,512]{2,1,0:T(8,128)}), f32[64,8,512]{2,1,0:T(8,128)}, u32[]{:S(2)}, u32[]{:S(2)}) async-start(f32[64,8,512]{2,1,0:T(8,128)} %get-tuple-element.19), calls=%async_computation | async-start | bytes 2097152 | tf_op jit(solution)/shard_map/all_to_all | solution.py:277
  47.3 38.9 %copy-start = (f32[6,512,8]{2,1,0:T(8,128)S(1)}, f32[6,512,8]{2,1,0:T(8,128)}, u32[]{:S(2)}) copy-start(f32[6,512,8]{2,1,0:T(8,128)} %fusion) | copy-start | bytes 294916
  104.5 1.2 copy-start.2
  105.7 5.9 %copy-start.1 = (f32[6,512,8]{2,1,0:T(8,128)S(1)}, f32[6,512,8]{2,1,0:T(8,128)}, u32[]{:S(2)}) copy-start(f32[6,512,8]{2,1,0:T(8,128)} %fusion) | copy-start | bytes 294916
  105.7 31.2 %all-to-all-start.2 = ((f32[64,8,512]{2,1,0:T(8,128)}), f32[64,8,512]{2,1,0:T(8,128)}, u32[]{:S(2)}, u32[]{:S(2)}) async-start(f32[64,8,512]{2,1,0:T(8,128)} %get-tuple-element.20), calls=%async_computation.2 | async-start | bytes 2097152 | tf_op jit(solution)/shard_map/all_to_all | solution.py:277
  110.1 1.7 copy-start.3
  136.8 30.8 %all-to-all-start.1 = ((f32[8,64,512]{2,0,1:T(8,128)}), f32[8,64,512]{2,0,1:T(8,128)}, u32[]{:S(2)}, u32[]{:S(2)}) async-start(f32[8,64,512]{2,0,1:T(8,128)} %copy.73), calls=%async_computation.1 | async-start | bytes 2097152 | tf_op jit(solution)/shard_map/all_to_all | solution.py:351
  142.6 1.4 copy-start.4
  167.7 30.1 %all-to-all-start.3 = ((f32[8,64,512]{2,0,1:T(8,128)}), f32[8,64,512]{2,0,1:T(8,128)S(1)}, u32[]{:S(2)}, u32[]{:S(2)}) async-start(f32[8,64,512]{2,0,1:T(8,128)} %copy.76), calls=%async_computation.3 | async-start | bytes 2097152 | tf_op jit(solution)/shard_map/all_to_all | solution.py:351

commit v5 on v4

--- a/solution.py
+++ b/solution.py
@@ -147,7 +147,7 @@
         q_ref[own, 1:2] = q / (reach * reach)
 
         def later(t, _):
-            at = pl.ds(pl.multiple_of(t * TILE, TILE), TILE)
+            at = pl.ds(pl.multiple_of(t * BLK, BLK), BLK)
             y = y_ref[:, at]
             cov = jnp.dot(ybt_ref[own, :], anomalies(y), preferred_element_type=jnp.float32)
             gap_r = prow_ref[0:1, at] - pcol_ref[own, 0:1]
@@ -158,8 +158,7 @@
             y_ref[:, at] = y + jnp.dot(dy_ref[:, own], gain, preferred_element_type=jnp.float32)
             return 0
 
-        per = BLK // TILE
-        lax.fori_loop((b + 1) * per, NBLK * per, later, 0)
+        lax.fori_loop(b + 1, NBLK, later, 0)
         return 0
 
     lax.fori_loop(0, NBLK, block, 0)
@@ -168,11 +167,11 @@
 def cells_kernel(
     n_tiles, first_col, base_ref, span_ref, x_ref, pcol_ref, ybt_ref, dy_ref, q_ref, out_ref, near_ref, across_ref
 ):
-    rows, members, cols = x_ref.shape
+    rows, members, cols = out_ref.shape
     base = base_ref[0].astype(jnp.float32)
-    out_ref[...] = x_ref[...]
+    out_ref[...] = x_ref[:, :, first_col : first_col + cols]
     groups = TILE // LANES
-    together = 4 if rows % 4 == 0 else 1
+    together = next(n for n in (8, 4, 2, 1) if rows % n == 0)
 
     def block(b, _):
         own = pl.ds(pl.multiple_of(b * BLK, BLK), BLK)
@@ -273,12 +272,7 @@
     tile_rows = local_rows // n_member
     first_row = base_row + lax.axis_index("member") * tile_rows
     width = cols // PARTS
-    cells = [
-        lax.all_to_all(
-            now[:, :, p * width : (p + 1) * width], "member", split_axis=0, concat_axis=1, tiled=True
-        )
-        for p in range(PARTS)
-    ]
+    cells = lax.all_to_all(now, "member", split_axis=0, concat_axis=1, tiled=True)
 
     local = row_i - base_row
     inside = (local >= 0) & (local < local_rows)
@@ -335,7 +329,7 @@
     for p in range(PARTS):
         result = pl.pallas_call(
             functools.partial(cells_kernel, cols // TILE, p * width),
-            out_shape=jax.ShapeDtypeStruct(cells[p].shape, f32),
+            out_shape=jax.ShapeDtypeStruct((tile_rows, members, width), f32),
             in_specs=[SMEM, SMEM] + [VMEM] * 5,
             out_specs=VMEM,
             scratch_shapes=[
@@ -346,7 +340,7 @@
             cost_estimate=pl.CostEstimate(
                 flops=2 * 10**10, bytes_accessed=10**7, transcendentals=0
             ),
-        )(jnp.reshape(first_row, (1,)).astype(jnp.int32), span, cells[p], by_obs, ybt, dy, q)
+        )(jnp.reshape(first_row, (1,)).astype(jnp.int32), span, cells, by_obs, ybt, dy, q)
         backs.append(
             lax.all_to_all(result, "member", split_axis=1, concat_axis=0, tiled=True)
         )

time: 200 us -> 180 us (0.900)
  Pallas kernels: 93.5 us -> 82.9 us
  local copies, waits for them, and re-layouts: 33.4 us -> 26.5 us
  starting transfers between devices: 23.5 us -> 19.2 us
  waiting for transfers between devices: 34.3 us -> 37.9 us
    pallas_call x2, Pallas kernels: 36.4 us -> 29.5 us  [on_device(): pl.pallas_call(functools.partial(cells_kernel, cols // TILE, p * width),...]
    pallas_call x1, Pallas kernels: 18.3 us -> 12.1 us  [on_device(): pl.pallas_call(observed_kernel, out_shape=[jax.ShapeDtypeStruct((n_obs, m...]
    all_to_all x2 -> x1, waiting for transfers between devices: 5.18 us -> 0.01 us  [on_device(): lax.all_to_all(now, 'member', split_axis=0, concat_axis=1, tiled=True)]
    ppermute x1, waiting for transfers between devices: 0.01 us -> 4.75 us  [forecast(): after = lax.ppermute(first, 'state', down)]
    gather x2, local copies, waits for them, and re-layouts: 12.9 us -> 8.55 us  [on_device(): jnp.take(table, block_order, axis=0)]
    all_to_all x2 -> x1, starting transfers between devices: 9.35 us -> 5.02 us  [on_device(): lax.all_to_all(now, 'member', split_axis=0, concat_axis=1, tiled=True)]
    all_to_all x2, waiting for transfers between devices: 29.1 us -> 31.7 us  [on_device(): lax.all_to_all(result, 'member', split_axis=1, concat_axis=0, tiled=True)]
    unnamed x33 -> x35, local copies, waits for them, and re-layouts: 7.06 us -> 8.27 us
  transfers between devices with their start and end apart: 6 -> 5, of which waited for: 3 -> 4; matrix products, arithmetic and copies ran while one was open for 17% -> 11% of each run, Pallas kernels for 47% -> 38%
where the time goes in v5:
time: 180 us; the launch traced here: 179 us
  Pallas kernels  82.9 us (46%)
  waiting for transfers between devices  37.9 us (21%)
  local copies, waits for them, and re-layouts  26.5 us (15%)
  starting transfers between devices  19.2 us (11%)
  other arithmetic  9.62 us (5%)
  matrix products  2.82 us (2%)
    all_to_all x2, waiting for transfers between devices, on_device(): lax.all_to_all(result, 'member', split_axis=1, concat_axis=0, tiled=True)  31.7 us
    pallas_call x2, Pallas kernels, on_device(): pl.pallas_call(functools.partial(cells_kernel, cols // TILE, p * width),...  29.5 us
    pallas_call x1, Pallas kernels, on_device(): pl.pallas_call(functools.partial(share_kernel, n_z, n_state), out_shape=j...  20.8 us
    pallas_call x1, Pallas kernels, on_device(): pl.pallas_call(pick_kernel, out_shape=jax.ShapeDtypeStruct((local_members...  20.5 us
    pallas_call x1, Pallas kernels, on_device(): pl.pallas_call(observed_kernel, out_shape=[jax.ShapeDtypeStruct((n_obs, m...  12.1 us
    gather x2, local copies, waits for them, and re-layouts, on_device(): jnp.take(table, block_order, axis=0)  8.55 us
    unnamed x35, local copies, waits for them, and re-layouts  8.27 us
    all_to_all x2, starting transfers between devices, on_device(): lax.all_to_all(result, 'member', split_axis=1, concat_axis=0, tiled=True)  8.03 us
  transfers between devices with their start and end apart: 5, of which 4 were waited for; matrix products, arithmetic and copies ran while one was open for 11% of the time, Pallas kernels for 38%

profile of v5, /device:TPU:0, one launch (start us, length us, event | category | flops | bytes accessed | tf_op | source)
XLA Modules:
  0.0 179.5 jit_solution(6065409425283576146)
XLA Ops:
  0.0 2.9 %copy.61 = f32[8,64,1024]{2,0,1:T(8,128)S(1)} copy(f32[8,64,1024]{2,1,0:T(8,128)} %param.8) | data formatting | bytes 4194304 | tf_op args[0]
  2.9 4.8 %collective-permute-start = (f32[9,2,1024]{2,0,1:T(8,128)S(1)}, f32[9,2,1024]{2,0,1:T(8,128)S(1)}, u32[]{:S(2)}, u32[]{:S(2)}) collective-permute-start(f32[9,2,1024]{2,0,1:T(8,128)S(1)} %pad_maximum_fusion.4), channel_id=1, source_target_pairs={{0,1},{1,2},{2,3},{4,5},{5,6},{6,7},{8,9},{9,10},{10,11},{12,13},{... | collective-permute-start | bytes 221192 | tf_op jit(solution)/shard_map/ppermute | solution.py:28
  9.1 1.4 collective-permute-done
  10.5 4.7 %collective-permute-done.1 = f32[9,2,1024]{2,0,1:T(8,128)S(1)} collective-permute-done((f32[9,2,1024]{2,0,1:T(8,128)S(1)}, f32[9,2,1024]{2,0,1:T(8,128)S(1)}, u32[]{:S(2)}, u32[]{:S(2)}) %collective-permute-start.1) | collective-permute-done | bytes 73760 | tf_op jit(solution)/shard_map/ppermute | solution.py:29
  16.5 1.3 fusion.5
  18.6 2.4 %fusion.10.field_ref = f32[64,8,1024]{2,1,0:T(8,128)} fusion(f32[8,66,1024]{2,0,1:T(8,128)S(1)} %fusion.5, f32[8,64,1023]{2,0,1:T(8,128)S(1)} %get-tuple-element.18, f32[8,64,1023]{2,0,1:T(8,128)S(1)} %get-tuple-element.17, f32[64,1024]{1,0:T(8,128)S(1)} %copy-done.8), kind=kLoop, calls=%fused_computation.16 | loop fusion | flops 3670016 | bytes 12840960 | tf_op jit(solution)/shard_map/transpose | solution.py:270
  21.0 5.0 %all-to-all-start = ((f32[64,8,1024]{2,1,0:T(8,128)}), f32[64,8,1024]{2,1,0:T(8,128)}, u32[]{:S(2)}, u32[]{:S(2)}) async-start(f32[64,8,1024]{2,1,0:T(8,128)} %fusion.10.field_ref), calls=%async_computation | async-start | bytes 4194304 | tf_op jit(solution)/shard_map/all_to_all | solution.py:275
  27.4 8.1 %gather_fusion = f32[3072,8]{1,0:T(8,128)S(1)} fusion(f32[3072,8]{1,0:T(8,128)S(1)} %copy.56, s32[3072]{0:T(1024)S(1)} %fusion.14), kind=kCustom, calls=%fused_computation | custom fusion | bytes 208896 | tf_op jit(solution)/shard_map/jit(_take)/gather | solution.py:265
  37.2 2.8 %fusion = f32[6,512,8]{2,1,0:T(8,128)S(1)} fusion(f32[6,512,8]{1,2,0:T(8,128)S(1)} %broadcast_select_fusion, s32[6,512]{1,0:T(8,128)S(1)} %convert_reduce_fusion), kind=kOutput, calls=%fused_computation.3 | convolution fusion | flops 152567808 | bytes 208896 | tf_op jit(solution)/shard_map/bpi,bif->bpf/dot_general | solution.py:237
  41.9 1.3 fusion.13
  43.2 20.5 %shard_map.82 = f32[8,3072]{1,0:T(8,128)S(1)} custom-call(s32[3072]{0:T(1024)S(1)} %get-tuple-element.24.where_ref, s32[3072]{0:T(1024)S(1)} %get-tuple-element.23.lane_ref, f32[64,8,1024]{2,1,0:T(8,128)} %fusion.10.field_ref), custom_call_target="tpu_custom_call" | custom-call | flops 10000000 | bytes 10000000 | tf_op jit(solution)/shard_map/pallas_call | solution.py:283
  63.7 20.8 %shard_map.83 = f32[2,4,4,8,768]{4,3,2,1,0:T(8,128)S(1)} custom-call(f32[4,8,768]{2,1,0:T(8,128)S(1)} %bitcast.97), custom_call_target="tpu_custom_call" | custom-call | tf_op jit(solution)/shard_map/pallas_call | solution.py:294
  84.6 12.1 %shard_map.84 = (bf16[3072,64]{1,0:T(8,128)(2,1)S(1)}, bf16[64,3072]{1,0:T(8,128)(2,1)S(1)}, f32[3072,8]{1,0:T(8,128)S(1)}) custom-call(f32[64,3072]{1,0:T(8,128)S(1)} %bitcast.96, f32[3072,8]{1,0:T(8,128)S(1)} %bitcast.90, f32[8,3072]{1,0:T(8,128)S(1)} %copy.69.prow_ref), custom_call_target="tpu_custom_call" | custom-call | flops 1000000000 | bytes 10000000 | tf_op jit(solution)/shard_map/pallas_call | solution.py:315
  98.4 1.9 %copy.88 = f32[8,8,8,1024]{3,2,0,1:T(8,128)S(1)} copy(f32[8,8,8,1024]{3,2,1,0:T(8,128)} %bitcast.10) | data formatting | bytes 4194304 | tf_op jit(solution)/shard_map/all_to_all | solution.py:275
  100.4 14.7 %shard_map.85 = f32[8,64,512]{2,1,0:T(8,128)S(1)} custom-call(s32[1]{0:T(128)} %bitcast.base_ref, s32[48]{0:T(128)S(1)} %reshape.185.span_ref, f32[8,64,1024]{2,1,0:T(8,128)S(1)} %bitcast.94, f32[3072,8]{1,0:T(8,128)S(1)} %bitcast.91, bf16[3072,64]{1,0:T(8,128)(2,1)S(1)} %copy-done.3, bf16[64,3072]{1,0:T(8,128)(2,1)S(1)} %copy-done.6, ...), custom_call_target="tpu_custom_call" | custom-call | flops 20000000000 | bytes 10000000 | tf_op jit(solution)/shard_map/pallas_call | solution.py:330
  115.2 1.6 copy.70
  116.8 4.5 %all-to-all-start.1 = ((f32[8,64,512]{2,0,1:T(8,128)}), f32[8,64,512]{2,0,1:T(8,128)}, u32[]{:S(2)}, u32[]{:S(2)}) async-start(f32[8,64,512]{2,0,1:T(8,128)} %copy.70), calls=%async_computation.1 | async-start | bytes 2097152 | tf_op jit(solution)/shard_map/all_to_all | solution.py:345
  121.2 1.6 copy-done.1
  125.0 14.7 %shard_map.86 = f32[8,64,512]{2,1,0:T(8,128)S(1)} custom-call(s32[1]{0:T(128)} %bitcast.base_ref, s32[48]{0:T(128)S(1)} %reshape.185.span_ref, f32[8,64,1024]{2,1,0:T(8,128)S(1)} %bitcast.95, f32[3072,8]{1,0:T(8,128)S(1)} %bitcast.92, bf16[3072,64]{1,0:T(8,128)(2,1)S(1)} %copy-done.4, bf16[64,3072]{1,0:T(8,128)(2,1)S(1)} %copy-done.7, ...), custom_call_target="tpu_custom_call" | custom-call | flops 20000000000 | bytes 10000000 | tf_op jit(solution)/shard_map/pallas_call | solution.py:330
  139.7 1.6 copy.72
  141.3 6.6 %all-to-all-done.1 = f32[8,64,512]{2,0,1:T(8,128)} async-done(((f32[8,64,512]{2,0,1:T(8,128)}), f32[8,64,512]{2,0,1:T(8,128)}, u32[]{:S(2)}, u32[]{:S(2)}) %all-to-all-start.1) | async-done | bytes 1048608 | tf_op jit(solution)/shard_map/all_to_all | solution.py:345
  147.8 3.6 %all-to-all-start.2 = ((f32[8,64,512]{2,0,1:T(8,128)}), f32[8,64,512]{2,0,1:T(8,128)S(1)}, u32[]{:S(2)}, u32[]{:S(2)}) async-start(f32[8,64,512]{2,0,1:T(8,128)} %copy.72), calls=%async_computation.2 | async-start | bytes 2097152 | tf_op jit(solution)/shard_map/all_to_all | solution.py:345
  152.7 25.2 %all-to-all-done.2 = f32[8,64,512]{2,0,1:T(8,128)S(1)} async-done(((f32[8,64,512]{2,0,1:T(8,128)}), f32[8,64,512]{2,0,1:T(8,128)S(1)}, u32[]{:S(2)}, u32[]{:S(2)}) %all-to-all-start.2) | async-done | bytes 1048608 | tf_op jit(solution)/shard_map/all_to_all | solution.py:345
  178.0 1.5 pad_maximum_fusion.1
  (79 shorter events, 13.3 us)
Async XLA Ops:
  0.0 2.9 %copy-start.8 = (f32[64,1024]{1,0:T(8,128)S(1)}, f32[64,1024]{1,0:T(8,128)}, u32[]{:S(2)}) copy-start(f32[64,1024]{1,0:T(8,128)} %param.9) | copy-start | bytes 786436
  2.9 7.6 %collective-permute-start = (f32[9,2,1024]{2,0,1:T(8,128)S(1)}, f32[9,2,1024]{2,0,1:T(8,128)S(1)}, u32[]{:S(2)}, u32[]{:S(2)}) collective-permute-start(f32[9,2,1024]{2,0,1:T(8,128)S(1)} %pad_maximum_fusion.4), channel_id=1, source_target_pairs={{0,1},{1,2},{2,3},{4,5},{5,6},{6,7},{8,9},{9,10},{10,11},{12,13},{... | collective-permute-start | bytes 221192 | tf_op jit(solution)/shard_map/ppermute | solution.py:28
  7.8 7.5 %collective-permute-start.1 = (f32[9,2,1024]{2,0,1:T(8,128)S(1)}, f32[9,2,1024]{2,0,1:T(8,128)S(1)}, u32[]{:S(2)}, u32[]{:S(2)}) collective-permute-start(f32[9,2,1024]{2,0,1:T(8,128)S(1)} %pad_maximum_fusion.5), channel_id=1, source_target_pairs={{1,0},{2,1},{3,2},{5,4},{6,5},{7,6},{9,8},{10,9},{11,10},{13,12},{... | collective-permute-start | bytes 221192 | tf_op jit(solution)/shard_map/ppermute | solution.py:29
  21.0 5.1 %copy-start.12 = (s32[3072]{0:T(1024)S(1)}, s32[3072]{0:T(1024)}, u32[]{:S(2)}) copy-start(s32[3072]{0:T(1024)} %param.12) | copy-start | bytes 36868
  21.0 5.1 %copy-start.13 = (s32[3072]{0:T(1024)S(1)}, s32[3072]{0:T(1024)}, u32[]{:S(2)}) copy-start(s32[3072]{0:T(1024)} %param.13) | copy-start | bytes 36868
  21.0 5.1 %copy-start.14 = (s32[3072]{0:T(1024)S(1)}, s32[3072]{0:T(1024)}, u32[]{:S(2)}) copy-start(s32[3072]{0:T(1024)} %param.14) | copy-start | bytes 36868
  21.0 5.8 %copy-start.10 = (f32[3072]{0:T(1024)S(1)}, f32[3072]{0:T(1024)}, u32[]{:S(2)}) copy-start(f32[3072]{0:T(1024)} %param.10) | copy-start | bytes 36868
  21.0 5.8 %copy-start.11 = (f32[3072]{0:T(1024)S(1)}, f32[3072]{0:T(1024)}, u32[]{:S(2)}) copy-start(f32[3072]{0:T(1024)} %param.11) | copy-start | bytes 36868
  21.0 6.4 %copy-start.9 = (s32[3072]{0:T(1024)S(1)}, s32[3072]{0:T(1024)}, u32[]{:S(2)}) copy-start(s32[3072]{0:T(1024)} %param.15) | copy-start | bytes 36868
  21.0 77.4 %all-to-all-start = ((f32[64,8,1024]{2,1,0:T(8,128)}), f32[64,8,1024]{2,1,0:T(8,128)}, u32[]{:S(2)}, u32[]{:S(2)}) async-start(f32[64,8,1024]{2,1,0:T(8,128)} %fusion.10.field_ref), calls=%async_computation | async-start | bytes 4194304 | tf_op jit(solution)/shard_map/all_to_all | solution.py:275
  96.8 0.9 copy-start.2
  97.7 0.8 copy-start.5
  98.4 1.9 %copy-start.3 = (bf16[3072,64]{1,0:T(8,128)(2,1)S(1)}, bf16[3072,64]{1,0:T(8,128)(2,1)}, u32[]{:S(2)}) copy-start(bf16[3072,64]{1,0:T(8,128)(2,1)} %copy-done.2) | copy-start | bytes 1179652
  98.4 2.0 %copy-start.6 = (bf16[64,3072]{1,0:T(8,128)(2,1)S(1)}, bf16[64,3072]{1,0:T(8,128)(2,1)}, u32[]{:S(2)}) copy-start(bf16[64,3072]{1,0:T(8,128)(2,1)} %copy-done.5) | copy-start | bytes 1179652
  100.4 14.8 %copy-start = (f32[8,8,8,1024]{3,2,0,1:T(8,128)}, f32[8,8,8,1024]{3,2,0,1:T(8,128)S(1)}, u32[]{:S(2)}) copy-start(f32[8,8,8,1024]{3,2,0,1:T(8,128)S(1)} %copy.88) | copy-start | bytes 6291460
  116.8 31.1 %all-to-all-start.1 = ((f32[8,64,512]{2,0,1:T(8,128)}), f32[8,64,512]{2,0,1:T(8,128)}, u32[]{:S(2)}, u32[]{:S(2)}) async-start(f32[8,64,512]{2,0,1:T(8,128)} %copy.70), calls=%async_computation.1 | async-start | bytes 2097152 | tf_op jit(solution)/shard_map/all_to_all | solution.py:345
  121.2 1.6 copy-start.1
  122.8 1.1 copy-start.4
  124.0 1.0 copy-start.7
  147.8 30.1 %all-to-all-start.2 = ((f32[8,64,512]{2,0,1:T(8,128)}), f32[8,64,512]{2,0,1:T(8,128)S(1)}, u32[]{:S(2)}, u32[]{:S(2)}) async-start(f32[8,64,512]{2,0,1:T(8,128)} %copy.72), calls=%async_computation.2 | async-start | bytes 2097152 | tf_op jit(solution)/shard_map/all_to_all | solution.py:345

commit v6 on v5

--- a/solution.py
+++ b/solution.py
@@ -40,24 +40,21 @@
     return current
 
 
-def pick_kernel(where_ref, lane_ref, field_ref, out_ref):
+def pick_kernel(where_ref, inside_ref, field_ref, out_ref):
     members = field_ref.shape[1]
     lane = lax.broadcasted_iota(jnp.int32, (members, LANES), 1)
 
     def chunk(j, _):
-        def step(t, acc):
-            for i in range(16):
-                k = j * LANES + t * 16 + i
-                packed = where_ref[k]
-                local = lax.shift_right_logical(packed, 15)
-                start = pl.multiple_of(packed & 0x7F80, LANES)
-                part = field_ref[local, :, pl.ds(start, LANES)]
-                turned = pltpu.roll(part, packed & (LANES - 1), 1)
-                acc = jnp.where(lane == lane_ref[k], turned, acc)
-            return acc
-
-        acc = lax.fori_loop(0, LANES // 16, step, jnp.zeros((members, LANES), jnp.float32))
-        out_ref[:, pl.ds(pl.multiple_of(j * LANES, LANES), LANES)] = acc
+        acc = jnp.zeros((members, LANES), jnp.float32)
+        for i in range(LANES):
+            packed = where_ref[j * LANES + i]
+            local = lax.shift_right_logical(packed, 15)
+            start = pl.multiple_of(packed & 0x7F80, LANES)
+            part = field_ref[local, :, pl.ds(start, LANES)]
+            turned = pltpu.roll(part, packed & (LANES - 1), 1)
+            acc = jnp.where(lane == i, turned, acc)
+        at = pl.ds(pl.multiple_of(j * LANES, LANES), LANES)
+        out_ref[:, at] = jnp.where(inside_ref[:, at] > 0, acc, 0.0)
         return 0
 
     lax.fori_loop(0, out_ref.shape[1] // LANES, chunk, 0)
@@ -279,11 +276,11 @@
     index = jnp.arange(n_obs, dtype=jnp.int32)
     turn = (index - col_i) & (LANES - 1)
     packed = (jnp.where(inside, local, 0) << 15) | (col_i & 0x7F80) | turn
-    target = jnp.where(inside, index & (LANES - 1), -1)
+    target = inside.astype(jnp.int32)[None, :]
     part = pl.pallas_call(
         pick_kernel,
         out_shape=jax.ShapeDtypeStruct((local_members, n_obs), f32),
-        in_specs=[SMEM, SMEM, VMEM],
+        in_specs=[SMEM, VMEM, VMEM],
         out_specs=VMEM,
         compiler_params=pltpu.CompilerParams(vmem_limit_bytes=32 * 1024 * 1024),
         cost_estimate=pl.CostEstimate(flops=10**7, bytes_accessed=10**7, transcendentals=0),

time: 180 us -> 180 us (level)
    pallas_call x1, Pallas kernels: 20.5 us -> 11.1 us  [on_device(): pl.pallas_call(pick_kernel, out_shape=jax.ShapeDtypeStruct((local_members...]
    pallas_call x1, Pallas kernels: 20.8 us -> 30 us  [on_device(): pl.pallas_call(functools.partial(share_kernel, n_z, n_state), out_shape=j...]
  transfers between devices with their start and end apart: 5 -> 5, of which waited for: 4 -> 4; matrix products, arithmetic and copies ran while one was open for 11% -> 12% of each run, Pallas kernels for 38% -> 38%
where the time goes in v6:
time: 180 us; the launch traced here: 179 us
  Pallas kernels  83 us (46%)
  waiting for transfers between devices  37.3 us (21%)
  local copies, waits for them, and re-layouts  26.9 us (15%)
  starting transfers between devices  19 us (11%)
  other arithmetic  9.91 us (6%)
  matrix products  2.82 us (2%)
    all_to_all x2, waiting for transfers between devices, on_device(): lax.all_to_all(result, 'member', split_axis=1, concat_axis=0, tiled=True)  31.8 us
    pallas_call x1, Pallas kernels, on_device(): pl.pallas_call(functools.partial(share_kernel, n_z, n_state), out_shape=j...  30 us
    pallas_call x2, Pallas kernels, on_device(): pl.pallas_call(functools.partial(cells_kernel, cols // TILE, p * width),...  29.7 us
    pallas_call x1, Pallas kernels, on_device(): pl.pallas_call(observed_kernel, out_shape=[jax.ShapeDtypeStruct((n_obs, m...  12.2 us
    pallas_call x1, Pallas kernels, on_device(): pl.pallas_call(pick_kernel, out_shape=jax.ShapeDtypeStruct((local_members...  11.1 us
    gather x2, local copies, waits for them, and re-layouts, on_device(): jnp.take(table, block_order, axis=0)  8.55 us
    unnamed x35, local copies, waits for them, and re-layouts  8.26 us
    all_to_all x2, starting transfers between devices, on_device(): lax.all_to_all(result, 'member', split_axis=1, concat_axis=0, tiled=True)  7.81 us
  transfers between devices with their start and end apart: 5, of which 4 were waited for; matrix products, arithmetic and copies ran while one was open for 12% of the time, Pallas kernels for 38%

profile of v6, /device:TPU:0, one launch (start us, length us, event | category | flops | bytes accessed | tf_op | source)
XLA Modules:
  0.0 179.4 jit_solution(16861694874795982324)
XLA Ops:
  0.0 2.9 %copy.83 = f32[8,64,1024]{2,0,1:T(8,128)S(1)} copy(f32[8,64,1024]{2,1,0:T(8,128)} %param.8) | data formatting | bytes 4194304 | tf_op args[0]
  2.9 4.8 %collective-permute-start = (f32[9,2,1024]{2,0,1:T(8,128)S(1)}, f32[9,2,1024]{2,0,1:T(8,128)S(1)}, u32[]{:S(2)}, u32[]{:S(2)}) collective-permute-start(f32[9,2,1024]{2,0,1:T(8,128)S(1)} %pad_maximum_fusion.4), channel_id=1, source_target_pairs={{0,1},{1,2},{2,3},{4,5},{5,6},{6,7},{8,9},{9,10},{10,11},{12,13},{... | collective-permute-start | bytes 221192 | tf_op jit(solution)/shard_map/ppermute | solution.py:28
  10.5 4.7 %collective-permute-done.1 = f32[9,2,1024]{2,0,1:T(8,128)S(1)} collective-permute-done((f32[9,2,1024]{2,0,1:T(8,128)S(1)}, f32[9,2,1024]{2,0,1:T(8,128)S(1)}, u32[]{:S(2)}, u32[]{:S(2)}) %collective-permute-start.1) | collective-permute-done | bytes 73760 | tf_op jit(solution)/shard_map/ppermute | solution.py:29
  16.5 1.3 fusion.5
  18.6 2.4 %fusion.10.field_ref = f32[64,8,1024]{2,1,0:T(8,128)} fusion(f32[8,66,1024]{2,0,1:T(8,128)S(1)} %fusion.5, f32[8,64,1023]{2,0,1:T(8,128)S(1)} %get-tuple-element.18, f32[8,64,1023]{2,0,1:T(8,128)S(1)} %get-tuple-element.17, f32[64,1024]{1,0:T(8,128)S(1)} %copy-done.8), kind=kLoop, calls=%fused_computation.16 | loop fusion | flops 3670016 | bytes 12840960 | tf_op jit(solution)/shard_map/transpose | solution.py:267
  21.0 5.0 %all-to-all-start = ((f32[64,8,1024]{2,1,0:T(8,128)}), f32[64,8,1024]{2,1,0:T(8,128)}, u32[]{:S(2)}, u32[]{:S(2)}) async-start(f32[64,8,1024]{2,1,0:T(8,128)} %fusion.10.field_ref), calls=%async_computation | async-start | bytes 4194304 | tf_op jit(solution)/shard_map/all_to_all | solution.py:272
  26.8 8.1 %gather_fusion = f32[3072,8]{1,0:T(8,128)S(1)} fusion(f32[3072,8]{1,0:T(8,128)S(1)} %copy.78, s32[3072]{0:T(1024)S(1)} %fusion.14), kind=kCustom, calls=%fused_computation | custom fusion | bytes 208896 | tf_op jit(solution)/shard_map/jit(_take)/gather | solution.py:262
  36.5 2.8 %fusion = f32[6,512,8]{2,1,0:T(8,128)S(1)} fusion(f32[6,512,8]{1,2,0:T(8,128)S(1)} %broadcast_select_fusion, s32[6,512]{1,0:T(8,128)S(1)} %convert_reduce_fusion), kind=kOutput, calls=%fused_computation.3 | convolution fusion | flops 152567808 | bytes 208896 | tf_op jit(solution)/shard_map/bpi,bif->bpf/dot_general | solution.py:234
  42.0 1.3 fusion.13
  43.4 11.1 %shard_map.82 = f32[8,3072]{1,0:T(8,128)S(1)} custom-call(s32[3072]{0:T(1024)S(1)} %and_or_fusion.where_ref, s32[1,3072]{1,0:T(1,128)S(1)} %copy.90.inside_ref, f32[64,8,1024]{2,1,0:T(8,128)} %fusion.10.field_ref), custom_call_target="tpu_custom_call" | custom-call | flops 10000000 | bytes 10000000 | tf_op jit(solution)/shard_map/pallas_call | solution.py:280
  54.5 30.0 %shard_map.83 = f32[2,4,4,8,768]{4,3,2,1,0:T(8,128)S(1)} custom-call(f32[4,8,768]{2,1,0:T(8,128)S(1)} %bitcast.98), custom_call_target="tpu_custom_call" | custom-call | tf_op jit(solution)/shard_map/pallas_call | solution.py:291
  84.6 12.2 %shard_map.84 = (bf16[3072,64]{1,0:T(8,128)(2,1)S(1)}, bf16[64,3072]{1,0:T(8,128)(2,1)S(1)}, f32[3072,8]{1,0:T(8,128)S(1)}) custom-call(f32[64,3072]{1,0:T(8,128)S(1)} %bitcast.97, f32[3072,8]{1,0:T(8,128)S(1)} %bitcast.91, f32[8,3072]{1,0:T(8,128)S(1)} %copy.92.prow_ref), custom_call_target="tpu_custom_call" | custom-call | flops 1000000000 | bytes 10000000 | tf_op jit(solution)/shard_map/pallas_call | solution.py:312
  98.4 1.9 %copy.111 = f32[8,8,8,1024]{3,2,0,1:T(8,128)S(1)} copy(f32[8,8,8,1024]{3,2,1,0:T(8,128)} %bitcast.10) | data formatting | bytes 4194304 | tf_op jit(solution)/shard_map/all_to_all | solution.py:272
  100.3 15.0 %shard_map.85 = f32[8,64,512]{2,1,0:T(8,128)S(1)} custom-call(s32[1]{0:T(128)} %bitcast.base_ref, s32[48]{0:T(128)S(1)} %reshape.185.span_ref, f32[8,64,1024]{2,1,0:T(8,128)S(1)} %bitcast.95, f32[3072,8]{1,0:T(8,128)S(1)} %bitcast.92, bf16[3072,64]{1,0:T(8,128)(2,1)S(1)} %copy-done.3, bf16[64,3072]{1,0:T(8,128)(2,1)S(1)} %copy-done.6, ...), custom_call_target="tpu_custom_call" | custom-call | flops 20000000000 | bytes 10000000 | tf_op jit(solution)/shard_map/pallas_call | solution.py:327
  115.3 1.6 copy.93
  116.9 4.3 %all-to-all-start.1 = ((f32[8,64,512]{2,0,1:T(8,128)}), f32[8,64,512]{2,0,1:T(8,128)}, u32[]{:S(2)}, u32[]{:S(2)}) async-start(f32[8,64,512]{2,0,1:T(8,128)} %copy.93), calls=%async_computation.1 | async-start | bytes 2097152 | tf_op jit(solution)/shard_map/all_to_all | solution.py:342
  121.2 1.6 copy-done.1
  124.9 14.7 %shard_map.86 = f32[8,64,512]{2,1,0:T(8,128)S(1)} custom-call(s32[1]{0:T(128)} %bitcast.base_ref, s32[48]{0:T(128)S(1)} %reshape.185.span_ref, f32[8,64,1024]{2,1,0:T(8,128)S(1)} %bitcast.96, f32[3072,8]{1,0:T(8,128)S(1)} %bitcast.93, bf16[3072,64]{1,0:T(8,128)(2,1)S(1)} %copy-done.4, bf16[64,3072]{1,0:T(8,128)(2,1)S(1)} %copy-done.7, ...), custom_call_target="tpu_custom_call" | custom-call | flops 20000000000 | bytes 10000000 | tf_op jit(solution)/shard_map/pallas_call | solution.py:327
  139.6 1.6 copy.95
  141.2 6.6 %all-to-all-done.1 = f32[8,64,512]{2,0,1:T(8,128)} async-done(((f32[8,64,512]{2,0,1:T(8,128)}), f32[8,64,512]{2,0,1:T(8,128)}, u32[]{:S(2)}, u32[]{:S(2)}) %all-to-all-start.1) | async-done | bytes 1048608 | tf_op jit(solution)/shard_map/all_to_all | solution.py:342
  147.8 3.6 %all-to-all-start.2 = ((f32[8,64,512]{2,0,1:T(8,128)}), f32[8,64,512]{2,0,1:T(8,128)S(1)}, u32[]{:S(2)}, u32[]{:S(2)}) async-start(f32[8,64,512]{2,0,1:T(8,128)} %copy.95), calls=%async_computation.2 | async-start | bytes 2097152 | tf_op jit(solution)/shard_map/all_to_all | solution.py:342
  151.3 1.3 copy.113
  152.7 25.2 %all-to-all-done.2 = f32[8,64,512]{2,0,1:T(8,128)S(1)} async-done(((f32[8,64,512]{2,0,1:T(8,128)}), f32[8,64,512]{2,0,1:T(8,128)S(1)}, u32[]{:S(2)}, u32[]{:S(2)}) %all-to-all-start.2) | async-done | bytes 1048608 | tf_op jit(solution)/shard_map/all_to_all | solution.py:342
  177.9 1.5 pad_maximum_fusion.1
  (81 shorter events, 13.5 us)
Async XLA Ops:
  0.0 2.9 %copy-start.8 = (f32[64,1024]{1,0:T(8,128)S(1)}, f32[64,1024]{1,0:T(8,128)}, u32[]{:S(2)}) copy-start(f32[64,1024]{1,0:T(8,128)} %param.9) | copy-start | bytes 786436
  0.0 9.1 %copy-start.12 = (s32[3072]{0:T(1024)S(1)}, s32[3072]{0:T(1024)}, u32[]{:S(2)}) copy-start(s32[3072]{0:T(1024)} %param.14) | copy-start | bytes 36868
  2.9 7.6 %collective-permute-start = (f32[9,2,1024]{2,0,1:T(8,128)S(1)}, f32[9,2,1024]{2,0,1:T(8,128)S(1)}, u32[]{:S(2)}, u32[]{:S(2)}) collective-permute-start(f32[9,2,1024]{2,0,1:T(8,128)S(1)} %pad_maximum_fusion.4), channel_id=1, source_target_pairs={{0,1},{1,2},{2,3},{4,5},{5,6},{6,7},{8,9},{9,10},{10,11},{12,13},{... | collective-permute-start | bytes 221192 | tf_op jit(solution)/shard_map/ppermute | solution.py:28
  7.8 7.5 %collective-permute-start.1 = (f32[9,2,1024]{2,0,1:T(8,128)S(1)}, f32[9,2,1024]{2,0,1:T(8,128)S(1)}, u32[]{:S(2)}, u32[]{:S(2)}) collective-permute-start(f32[9,2,1024]{2,0,1:T(8,128)S(1)} %pad_maximum_fusion.5), channel_id=1, source_target_pairs={{1,0},{2,1},{3,2},{5,4},{6,5},{7,6},{9,8},{10,9},{11,10},{13,12},{... | collective-permute-start | bytes 221192 | tf_op jit(solution)/shard_map/ppermute | solution.py:29
  21.0 5.0 %copy-start.9 = (s32[3072]{0:T(1024)S(1)}, s32[3072]{0:T(1024)}, u32[]{:S(2)}) copy-start(s32[3072]{0:T(1024)} %param.15) | copy-start | bytes 36868
  21.0 5.1 %copy-start.13 = (s32[3072]{0:T(1024)S(1)}, s32[3072]{0:T(1024)}, u32[]{:S(2)}) copy-start(s32[3072]{0:T(1024)} %param.12) | copy-start | bytes 36868
  21.0 5.1 %copy-start.14 = (s32[3072]{0:T(1024)S(1)}, s32[3072]{0:T(1024)}, u32[]{:S(2)}) copy-start(s32[3072]{0:T(1024)} %param.13) | copy-start | bytes 36868
  21.0 5.1 %copy-start.10 = (f32[3072]{0:T(1024)S(1)}, f32[3072]{0:T(1024)}, u32[]{:S(2)}) copy-start(f32[3072]{0:T(1024)} %param.10) | copy-start | bytes 36868
  21.0 5.1 %copy-start.11 = (f32[3072]{0:T(1024)S(1)}, f32[3072]{0:T(1024)}, u32[]{:S(2)}) copy-start(f32[3072]{0:T(1024)} %param.11) | copy-start | bytes 36868
  21.0 77.4 %all-to-all-start = ((f32[64,8,1024]{2,1,0:T(8,128)}), f32[64,8,1024]{2,1,0:T(8,128)}, u32[]{:S(2)}, u32[]{:S(2)}) async-start(f32[64,8,1024]{2,1,0:T(8,128)} %fusion.10.field_ref), calls=%async_computation | async-start | bytes 4194304 | tf_op jit(solution)/shard_map/all_to_all | solution.py:272
  96.7 0.9 copy-start.2
  97.6 0.7 copy-start.5
  98.4 1.9 %copy-start.3 = (bf16[3072,64]{1,0:T(8,128)(2,1)S(1)}, bf16[3072,64]{1,0:T(8,128)(2,1)}, u32[]{:S(2)}) copy-start(bf16[3072,64]{1,0:T(8,128)(2,1)} %copy-done.2) | copy-start | bytes 1179652
  98.4 2.0 %copy-start.6 = (bf16[64,3072]{1,0:T(8,128)(2,1)S(1)}, bf16[64,3072]{1,0:T(8,128)(2,1)}, u32[]{:S(2)}) copy-start(bf16[64,3072]{1,0:T(8,128)(2,1)} %copy-done.5) | copy-start | bytes 1179652
  100.3 15.0 %copy-start = (f32[8,8,8,1024]{3,2,0,1:T(8,128)}, f32[8,8,8,1024]{3,2,0,1:T(8,128)S(1)}, u32[]{:S(2)}) copy-start(f32[8,8,8,1024]{3,2,0,1:T(8,128)S(1)} %copy.111) | copy-start | bytes 6291460
  116.9 30.9 %all-to-all-start.1 = ((f32[8,64,512]{2,0,1:T(8,128)}), f32[8,64,512]{2,0,1:T(8,128)}, u32[]{:S(2)}, u32[]{:S(2)}) async-start(f32[8,64,512]{2,0,1:T(8,128)} %copy.93), calls=%async_computation.1 | async-start | bytes 2097152 | tf_op jit(solution)/shard_map/all_to_all | solution.py:342
  121.2 1.6 copy-start.1
  122.8 1.1 copy-start.4
  123.9 1.0 copy-start.7
  147.8 30.1 %all-to-all-start.2 = ((f32[8,64,512]{2,0,1:T(8,128)}), f32[8,64,512]{2,0,1:T(8,128)S(1)}, u32[]{:S(2)}, u32[]{:S(2)}) async-start(f32[8,64,512]{2,0,1:T(8,128)} %copy.95), calls=%async_computation.2 | async-start | bytes 2097152 | tf_op jit(solution)/shard_map/all_to_all | solution.py:342
